TPU v7x, 256 devices: a whole 4x4x8 slice. The times are simulated.
256 devices in a mesh: seq: 64 (over y_hi, z, x), chan: 4 (over y_lo, core).
Axes of the slice: x: 4, y: 4 (y_hi: 2, y_lo: 2; y = y_hi * 2 + y_lo), z: 8, core: 2. Of those that a mesh axis runs over, the one named last changes fastest.
Arguments:
- activation: bfloat16 [262144, 1024], P('seq', 'chan'), may hold values from -6 to 6
- gating: bfloat16 [262144, 1024], P('seq', 'chan'), may hold values from -6 to 6
- kernel_diag: bfloat16 [262144, 1024], P('seq', 'chan'), may hold values from -6 to 6
- cotangent: bfloat16 [262144, 1024], P('seq', 'chan'), may hold values from -6 to 6
- factor_right: bfloat16 [512, 512], replicated, may hold values from -0.25 to 0.25
- factor_left: bfloat16 [512, 512], replicated, may hold values from -0.25 to 0.25
- projection: bfloat16 [1024, 1024], P('chan'), may hold values from -0.1875 to 0.1875
Outputs:
- input_grad: bfloat16 [262144, 1024], P('seq', 'chan')
- projection_grad: float32 [1024, 1024], P('chan', 'seq')
- right_grad: float32 [512, 512], P('seq', 'chan')
- left_grad: float32 [512, 512], P('seq', 'chan')
All inputs are finite; a program needn't handle non-finite values.
Results may differ from a plain program's by a relative error of at most 0.0064.
Values may be sent and summed in bfloat16 or wider, within the bound.
A program may use at most 128 MiB of HBM per device.

v0:
```python
import jax
import jax.numpy as jnp
from jax import lax
from jax.sharding import PartitionSpec as P


def contract_rows(left_side, right_side):
    return lax.dot_general(
        left_side, right_side, (((0,), (0,)), ((), ())), preferred_element_type=jnp.float32
    )


def contract_cols(left_side, right_side):
    return lax.dot_general(
        left_side, right_side, (((1,), (1,)), ((), ())), preferred_element_type=jnp.float32
    )


def on_device(activation, gating, kernel_diag, cotangent, factor_right, factor_left, projection):
    row_count, chan_count = activation.shape
    block_size = factor_right.shape[0]
    local_blocks = row_count // block_size
    full_width = projection.shape[1]
    cube_shape = (local_blocks, block_size, chan_count)
    values = (
        (activation.astype(jnp.float32) * gating.astype(jnp.float32))
        .astype(jnp.bfloat16)
        .reshape(cube_shape)
    )
    kernel_cube = kernel_diag.astype(jnp.float32).reshape(cube_shape)
    first_out = jnp.einsum("kj,ijd->ikd", factor_right, values, preferred_element_type=jnp.float32)
    scaled = (first_out * kernel_cube).astype(jnp.bfloat16)
    received = lax.all_to_all(scaled, "seq", split_axis=1, concat_axis=0, tiled=True)
    mixed_piece = jnp.einsum(
        "mi,ikd->kmd", factor_left, received, preferred_element_type=jnp.float32
    )
    mixed_out = mixed_piece.astype(jnp.bfloat16)
    mixed_flat = mixed_out.reshape(row_count, chan_count)
    portion = lax.all_gather(cotangent, "chan", axis=1, tiled=True)
    grad_total = contract_cols(portion, projection)
    updated = contract_rows(mixed_flat, portion)
    mixed_grad = grad_total.astype(jnp.bfloat16)
    projection_grad = lax.psum_scatter(updated, "seq", scatter_dimension=1, tiled=True) / block_size
    upstream = mixed_grad.reshape(cube_shape)
    left_part = jnp.einsum("kmd,ikd->mi", upstream, received, preferred_element_type=jnp.float32)
    scaled_grad_out = jnp.einsum(
        "mi,kmd->ikd", factor_left, upstream, preferred_element_type=jnp.float32
    ).astype(jnp.bfloat16)
    scaled_grad = lax.all_to_all(scaled_grad_out, "seq", split_axis=0, concat_axis=1, tiled=True)
    first_grad = (scaled_grad.astype(jnp.float32) * kernel_cube).astype(jnp.bfloat16)
    right_part = jnp.einsum("ikd,ijd->kj", first_grad, values, preferred_element_type=jnp.float32)
    values_grad = jnp.einsum(
        "kj,ikd->ijd", factor_right, first_grad, preferred_element_type=jnp.float32
    )
    input_grad = (
        (values_grad * gating.astype(jnp.float32).reshape(cube_shape))
        .astype(jnp.bfloat16)
        .reshape(row_count, chan_count)
    )
    grad_scale = (block_size * full_width) ** (-0.5)
    right_total, left_total = lax.psum((right_part, left_part), ("seq", "chan"))
    row_share = block_size // lax.axis_size("seq")
    col_share = block_size // lax.axis_size("chan")
    row_start = lax.axis_index("seq") * row_share
    col_start = lax.axis_index("chan") * col_share
    right_grad = lax.dynamic_slice(right_total, (row_start, col_start), (row_share, col_share))
    left_grad = lax.dynamic_slice(left_total, (row_start, col_start), (row_share, col_share))
    return (input_grad, projection_grad, right_grad * grad_scale, left_grad * grad_scale)


def solution(mesh):
    in_specs = (
        P("seq", "chan"),
        P("seq", "chan"),
        P("seq", "chan"),
        P("seq", "chan"),
        P(),
        P(),
        P("chan", None),
    )
    out_specs = (P("seq", "chan"), P("chan", "seq"), P("seq", "chan"), P("seq", "chan"))
    return jax.shard_map(
        on_device, mesh=mesh, in_specs=in_specs, out_specs=out_specs, check_vma=False
    )
```

profile of v0, /device:TPU:1, one launch (start us, length us, event | category | flops | bytes accessed | tf_op | source)
XLA Modules:
  0.0 800.2 jit_solution(5401588785874761612)
XLA Ops:
  7.2 0.0 all-gather.2.cloned.1.call-start
  7.2 0.7 all-gather.2.cloned.1.call-update
  7.9 4.3 copy.37
  12.2 2.3 multiply_convert_fusion
  14.5 1.3 copy-done.3
  15.9 2.6 fusion
  18.5 4.6 copy.38
  23.1 15.4 %all-to-all-start.1 = ((bf16[8,512,256]{2,0,1:T(8,128)(2,1)}), bf16[8,512,256]{2,0,1:T(8,128)(2,1)}, u32[]{:S(2)}, u32[]{:S(2)}) async-start(bf16[8,512,256]{2,0,1:T(8,128)(2,1)} %copy.38), calls=%async_computation.1 | async-start | bytes 4194304 | tf_op jit(solution)/shard_map/all_to_all | solution.py:33
  38.4 82.0 %all-gather.2.cloned.1.call-done = bf16[4096,1024]{1,0:T(8,128)(2,1)} async-done(((bf16[4096,256]{1,0:T(8,128)(2,1)}), bf16[4096,1024]{1,0:T(8,128)(2,1)}) %all-gather.2.cloned.1.call-update) | async-done | bytes 8388624 | tf_op jit(solution)/shard_map/all_gather | solution.py:39
  120.4 5.8 convolution_convert_fusion
  126.2 1.3 copy-done.6
  127.5 2.6 convert_bitcast_fusion.2
  130.1 4.5 copy.31
  134.6 12.6 %all-to-all-start = ((bf16[512,8,256]{2,1,0:T(8,128)(2,1)}), bf16[512,8,256]{2,1,0:T(8,128)(2,1)}, u32[]{:S(2)}, u32[]{:S(2)}) async-start(bf16[512,8,256]{2,1,0:T(8,128)(2,1)} %copy.31), calls=%async_computation | async-start | bytes 4194304 | tf_op jit(solution)/shard_map/all_to_all | solution.py:49
  147.2 0.2 reduce-scatter.2.cloned.1.call-start
  147.5 2.3 copy.40
  149.7 1.3 copy-done.4
  151.1 2.7 convert_bitcast_fusion.1
  153.8 3.9 copy.42
  157.7 8.3 %fusion.15 = f32[256,1024]{0,1:T(8,128)} fusion(bf16[4096,256]{1,0:T(8,128)(2,1)} %bitcast.69, bf16[4096,1024]{1,0:T(8,128)(2,1)} %all-gather.2.cloned.1.call-done), kind=kOutput, calls=%fused_computation.23 | convolution fusion | flops 2147483648 | bytes 11534336 | tf_op jit(solution)/shard_map/dot_general | solution.py:8
  166.0 0.0 reduce-scatter.2.cloned.1.call-update
  166.1 0.0 all-reduce.3.cloned.1.call-start
  166.1 4.5 fusion.6
  170.6 28.7 %all-to-all-done = bf16[512,8,256]{2,1,0:T(8,128)(2,1)} async-done(((bf16[512,8,256]{2,1,0:T(8,128)(2,1)}), bf16[512,8,256]{2,1,0:T(8,128)(2,1)}, u32[]{:S(2)}, u32[]{:S(2)}) %all-to-all-start) | async-done | bytes 2097184 | tf_op jit(solution)/shard_map/all_to_all | solution.py:49
  199.4 5.2 convolution_bitcast_fusion
  204.5 2.9 copy.34
  207.4 273.4 %reduce-scatter.2.cloned.1.call-done = f32[256,16]{0,1:T(8,128)} async-done(((f32[256,1024]{0,1:T(8,128)}), f32[256,16]{0,1:T(8,128)}) %reduce-scatter.2.cloned.1.call-update) | async-done | bytes 16400 | tf_op jit(solution)/shard_map/reduce_scatter | solution.py:43
  480.8 1.3 broadcast_multiply_fusion
  482.1 4.8 fusion.1
  486.9 2.4 copy.35
  489.3 303.1 %all-reduce.3.cloned.1.call-done = (f32[512,512]{1,0:T(8,128)}, f32[512,512]{1,0:T(8,128)}) async-done(((f32[512,512]{1,0:T(8,128)}, f32[512,512]{1,0:T(8,128)}), (f32[512,512]{1,0:T(8,128)}, f32[512,512]{1,0:T(8,128)})) %all-reduce.3.cloned.1.call-update) | async-done | bytes 2097168 | tf_op jit(solution)/shard_map/psum | solution.py:61
  792.4 1.3 dynamic-slice_multiply_fusion
  (13 shorter events, 0.0 us)
Async XLA Ops:
  7.2 120.4 %copy-start = (bf16[512,512]{1,0:T(8,128)(2,1)S(1)}, bf16[512,512]{1,0:T(8,128)(2,1)}, u32[]{:S(2)}) copy-start(bf16[512,512]{1,0:T(8,128)(2,1)} %param.12) | copy-start | bytes 1572868
  7.2 113.2 %all-gather.2.cloned.1.call-start = ((), (), s32[]{:S(2)}) async-start(), calls=%async_computation.3 | async-start | bytes 10485760 | tf_op jit(solution)/shard_map/all_gather | solution.py:39
  7.9 4.3 copy-start.2
  12.2 3.6 copy-start.1
  12.2 3.6 copy-start.5
  14.5 1.3 copy-start.3
  23.1 111.6 %all-to-all-start.1 = ((bf16[8,512,256]{2,0,1:T(8,128)(2,1)}), bf16[8,512,256]{2,0,1:T(8,128)(2,1)}, u32[]{:S(2)}, u32[]{:S(2)}) async-start(bf16[8,512,256]{2,0,1:T(8,128)(2,1)} %copy.38), calls=%async_computation.1 | async-start | bytes 4194304 | tf_op jit(solution)/shard_map/all_to_all | solution.py:33
  126.2 1.3 copy-start.6
  134.6 64.7 %all-to-all-start = ((bf16[512,8,256]{2,1,0:T(8,128)(2,1)}), bf16[512,8,256]{2,1,0:T(8,128)(2,1)}, u32[]{:S(2)}, u32[]{:S(2)}) async-start(bf16[512,8,256]{2,1,0:T(8,128)(2,1)} %copy.31), calls=%async_computation | async-start | bytes 4194304 | tf_op jit(solution)/shard_map/all_to_all | solution.py:49
  147.2 333.6 %reduce-scatter.2.cloned.1.call-start = ((), (), s32[]{:S(2)}) async-start(), calls=%async_computation.4 | async-start | bytes 1064960 | tf_op jit(solution)/shard_map/reduce_scatter | solution.py:43
  149.7 1.3 copy-start.4
  166.1 626.4 %all-reduce.3.cloned.1.call-start = ((), (), s32[]{:S(2)}) async-start(), calls=%async_computation.5 | async-start | bytes 4194304 | tf_op jit(solution)/shard_map/psum | solution.py:61
Sparse Core Ops, SparseCore 0:
  9.8 110.5 all-gather.1
  166.2 314.5 reduce-scatter.1
  487.3 305.0 all-reduce.2
where the time goes:
time: 802 us; the launch traced here: 800 us
  waiting for transfers between devices  688 us (86%)
  matrix products  36.5 us (5%)
  local copies, waits for them, and re-layouts  28.8 us (4%)
  starting transfers between devices  28.3 us (4%)
  between operations  13.8 us (2%)
    psum x1, waiting for transfers between devices, on_device(): right_total, left_total = lax.psum((right_part, left_part), ('seq', 'chan'))  303 us
    reduce_scatter x1, waiting for transfers between devices, on_device(): lax.psum_scatter(updated, 'seq', scatter_dimension=1, tiled=True)  273 us
    all_gather x1, waiting for transfers between devices, on_device(): portion = lax.all_gather(cotangent, 'chan', axis=1, tiled=True)  82 us
    all_to_all x1, waiting for transfers between devices, on_device(): lax.all_to_all(scaled_grad_out, 'seq', split_axis=0, concat_axis=1, tiled...  28.7 us
  transfers between devices with their start and end apart: 5, of which 4 were waited for; matrix products, arithmetic and copies ran while one was open for 8% of the time, Pallas kernels for 0%

commit v1 on v0

v1 whole, which is shorter than its diff:
```python
import jax
import jax.numpy as jnp
from jax import lax
from jax.sharding import PartitionSpec as P


def on_device(activation, gating, kernel_diag, cotangent, factor_right, factor_left, projection):
    row_count, chan_count = activation.shape
    block_size = factor_right.shape[0]
    local_blocks = row_count // block_size
    full_width = projection.shape[1]
    seq_size = lax.axis_size("seq")
    chan_size = lax.axis_size("chan")
    cube_shape = (local_blocks, block_size, chan_count)
    my_chan = lax.axis_index("chan")

    def swap(array, bit):
        return lax.ppermute(array, "chan", [(c, c ^ bit) for c in range(chan_size)])

    from_far = swap(cotangent, 2)
    from_sibling = swap(cotangent, 1)
    from_far_sibling = swap(from_far, 1)
    pieces = (cotangent, from_sibling, from_far, from_far_sibling)

    values = (
        (activation.astype(jnp.float32) * gating.astype(jnp.float32))
        .astype(jnp.bfloat16)
        .reshape(cube_shape)
    )
    kernel_cube = kernel_diag.astype(jnp.float32).reshape(cube_shape)
    first_out = jnp.einsum("kj,ijd->ikd", factor_right, values, preferred_element_type=jnp.float32)
    scaled = (first_out * kernel_cube).astype(jnp.bfloat16)
    received = lax.all_to_all(scaled, "seq", split_axis=1, concat_axis=0, tiled=True)

    order = my_chan ^ jnp.arange(chan_size)
    proj_blocks = projection.reshape(chan_count, chan_size, chan_count)
    proj_mine = jnp.take(proj_blocks, order, axis=1).reshape(chan_count, full_width)
    portion = jnp.concatenate(pieces, axis=1)
    grad_total = lax.dot_general(
        portion, proj_mine, (((1,), (1,)), ((), ())), preferred_element_type=jnp.float32
    )
    upstream = grad_total.astype(jnp.bfloat16).reshape(cube_shape)
    scaled_grad_out = jnp.einsum(
        "mi,kmd->ikd", factor_left, upstream, preferred_element_type=jnp.float32
    ).astype(jnp.bfloat16)
    scaled_grad = lax.all_to_all(scaled_grad_out, "seq", split_axis=0, concat_axis=1, tiled=True)

    mixed_flat = (
        jnp.einsum("mi,ikd->kmd", factor_left, received, preferred_element_type=jnp.float32)
        .astype(jnp.bfloat16)
        .reshape(row_count, chan_count)
    )
    updated = lax.dot_general(
        mixed_flat, portion, (((0,), (0,)), ((), ())), preferred_element_type=jnp.float32
    )
    updated = jnp.take(
        updated.reshape(chan_count, chan_size, chan_count), order, axis=1
    ).reshape(chan_count, full_width)
    left_part = jnp.einsum("kmd,ikd->mi", upstream, received, preferred_element_type=jnp.float32)

    first_grad = (scaled_grad.astype(jnp.float32) * kernel_cube).astype(jnp.bfloat16)
    right_part = jnp.einsum("ikd,ijd->kj", first_grad, values, preferred_element_type=jnp.float32)
    values_grad = jnp.einsum(
        "kj,ikd->ijd", factor_right, first_grad, preferred_element_type=jnp.float32
    )
    input_grad = (
        (values_grad * gating.astype(jnp.float32).reshape(cube_shape))
        .astype(jnp.bfloat16)
        .reshape(row_count, chan_count)
    )

    grad_scale = (block_size * full_width) ** (-0.5)
    row_share = block_size // seq_size
    col_share = block_size // chan_size
    out_share = full_width // seq_size

    def over_chan(part):
        blocks = part.astype(jnp.bfloat16).reshape(block_size, chan_size, col_share)
        blocks = blocks.transpose(1, 0, 2)
        arrived = lax.all_to_all(blocks, "chan", split_axis=0, concat_axis=0, tiled=True)
        return jnp.sum(arrived.astype(jnp.float32), axis=0)

    def over_seq(blocks):
        arrived = lax.all_to_all(
            blocks.astype(jnp.bfloat16), "seq", split_axis=0, concat_axis=0, tiled=True
        )
        return jnp.sum(arrived.astype(jnp.float32), axis=0)

    proj_rows = updated.reshape(chan_count, seq_size, out_share).transpose(1, 0, 2)
    proj_rows = proj_rows.reshape(seq_size, -1, col_share)
    left_rows = over_chan(left_part).reshape(seq_size, row_share, col_share)
    early = over_seq(jnp.concatenate([proj_rows, left_rows], axis=1))
    proj_count = proj_rows.shape[1]
    projection_grad = early[:proj_count].reshape(chan_count, out_share) / block_size
    left_grad = early[proj_count:] * grad_scale
    right_rows = over_chan(right_part).reshape(seq_size, row_share, col_share)
    right_grad = over_seq(right_rows) * grad_scale
    return (input_grad, projection_grad, right_grad, left_grad)


def solution(mesh):
    in_specs = (
        P("seq", "chan"),
        P("seq", "chan"),
        P("seq", "chan"),
        P("seq", "chan"),
        P(),
        P(),
        P("chan", None),
    )
    out_specs = (P("seq", "chan"), P("chan", "seq"), P("seq", "chan"), P("seq", "chan"))
    return jax.shard_map(
        on_device, mesh=mesh, in_specs=in_specs, out_specs=out_specs, check_vma=False
    )
```

time: 802 us -> 298 us (0.37)
  waiting for transfers between devices: 688 us -> 129 us
  local copies, waits for them, and re-layouts: 28.8 us -> 67.1 us
  starting transfers between devices: 28.3 us -> 55.2 us
  between operations: 13.8 us -> 0.85 us
    psum x1 -> x0, waiting for transfers between devices: 303 us -> none  [on_device(): right_total, left_total = lax.psum((right_part, left_part), ('seq', 'chan'))]
    reduce_scatter x1 -> x0, waiting for transfers between devices: 273 us -> none  [on_device(): lax.psum_scatter(updated, 'seq', scatter_dimension=1, tiled=True)]
    all_gather x1 -> x0, waiting for transfers between devices: 82 us -> none  [on_device(): portion = lax.all_gather(cotangent, 'chan', axis=1, tiled=True)]
    ppermute x0 -> x3, waiting for transfers between devices: none -> 62.9 us  [swap(): return lax.ppermute(array, 'chan', [(c, c ^ bit) for c in range(chan_size)])]
    all_to_all x0 -> x4, starting transfers between devices: none -> 30 us  [the longest x2 18.2 us: over_seq(): lax.all_to_all(blocks.astype(jnp.bfloat16), 'seq', split_axis=0, concat_a...]
    all_to_all x0 -> x4, waiting for transfers between devices: none -> 20.1 us  [the longest x2 13.5 us: over_seq(): lax.all_to_all(blocks.astype(jnp.bfloat16), 'seq', split_axis=0, concat_a...]
    all_to_all x1, waiting for transfers between devices: 28.7 us -> 45.5 us  [on_device(): lax.all_to_all(scaled_grad_out, 'seq', split_axis=0, concat_axis=1, tiled...]
    dot_general x0 -> x1, local copies, waits for them, and re-layouts: none -> 11.4 us  [on_device(): lax.dot_general(mixed_flat, portion, (((0,), (0,)), ((), ())), preferred_...]
  transfers between devices with their start and end apart: 5 -> 9, of which waited for: 4 -> 5; matrix products, arithmetic and copies ran while one was open for 8% -> 24% of each run, Pallas kernels for 0% -> 0%
where the time goes in v1:
time: 298 us; the launch traced here: 297 us
  waiting for transfers between devices  129 us (43%)
  local copies, waits for them, and re-layouts  67.1 us (23%)
  starting transfers between devices  55.2 us (19%)
  matrix products  35.3 us (12%)
  other arithmetic  9.67 us (3%)
    ppermute x3, waiting for transfers between devices, swap(): return lax.ppermute(array, 'chan', [(c, c ^ bit) for c in range(chan_size)])  62.9 us
    all_to_all x1, waiting for transfers between devices, on_device(): lax.all_to_all(scaled_grad_out, 'seq', split_axis=0, concat_axis=1, tiled...  45.5 us
    all_to_all x2, starting transfers between devices, over_seq(): lax.all_to_all(blocks.astype(jnp.bfloat16), 'seq', split_axis=0, concat_a...  18.2 us
    all_to_all x1, starting transfers between devices, on_device(): lax.all_to_all(scaled, 'seq', split_axis=1, concat_axis=0, tiled=True)  15.5 us
    unnamed x27, local copies, waits for them, and re-layouts  13.8 us
    all_to_all x2, waiting for transfers between devices, over_seq(): lax.all_to_all(blocks.astype(jnp.bfloat16), 'seq', split_axis=0, concat_a...  13.5 us
    all_to_all x2, starting transfers between devices, over_chan(): lax.all_to_all(blocks, 'chan', split_axis=0, concat_axis=0, tiled=True)  11.8 us
    dot_general x1, local copies, waits for them, and re-layouts, on_device(): lax.dot_general(mixed_flat, portion, (((0,), (0,)), ((), ())), preferred_...  11.4 us
  transfers between devices with their start and end apart: 9, of which 5 were waited for; matrix products, arithmetic and copies ran while one was open for 24% of the time, Pallas kernels for 0%

profile of v1, /device:TPU:1, one launch (start us, length us, event | category | flops | bytes accessed | tf_op | source)
XLA Modules:
  0.0 296.8 jit_solution(16274715010552303804)
XLA Ops:
  0.7 4.3 %copy.93 = f32[8,512,256]{1,2,0:T(8,128)} copy(bf16[8,512,256]{2,1,0:T(8,128)(2,1)} %bitcast.91) | data formatting | bytes 6291456 | tf_op jit(solution)/shard_map/reshape | solution.py:30
  4.9 2.3 multiply_convert_fusion
  8.6 2.6 fusion
  11.2 4.5 %copy.94 = bf16[8,512,256]{2,0,1:T(8,128)(2,1)} copy(bf16[8,512,256]{1,2,0:T(8,128)(2,1)} %fusion) | data formatting | bytes 4194304 | tf_op jit(solution)/shard_map/convert_element_type | solution.py:32
  15.7 15.5 %all-to-all-start.1 = ((bf16[8,512,256]{2,0,1:T(8,128)(2,1)}), bf16[8,512,256]{2,0,1:T(8,128)(2,1)}, u32[]{:S(2)}, u32[]{:S(2)}) async-start(bf16[8,512,256]{2,0,1:T(8,128)(2,1)} %copy.94), calls=%async_computation.1 | async-start | bytes 4194304 | tf_op jit(solution)/shard_map/all_to_all | solution.py:33
  38.1 62.9 %collective-permute-done.1 = bf16[4096,256]{1,0:T(8,128)(2,1)} collective-permute-done((bf16[4096,256]{1,0:T(8,128)(2,1)}, bf16[4096,256]{1,0:T(8,128)(2,1)}, u32[]{:S(2)}, u32[]{:S(2)}) %collective-permute-start.1) | collective-permute-done | bytes 2097184 | tf_op jit(solution)/shard_map/ppermute | solution.py:18
  102.8 3.2 %constant_dynamic-update-slice_fusion.3 = bf16[4096,1024]{1,0:T(8,128)(2,1)} fusion(bf16[4096,256]{1,0:T(8,128)(2,1)} %param.10), kind=kLoop, calls=%fused_computation.34 | loop fusion | bytes 4194304
  106.0 3.1 %constant_dynamic-update-slice_fusion.2 = bf16[4096,1024]{1,0:T(8,128)(2,1)} fusion(bf16[4096,1024]{1,0:T(8,128)(2,1)} %constant_dynamic-update-slice_fusion.3, bf16[4096,256]{1,0:T(8,128)(2,1)} %collective-permute-done), kind=kLoop, calls=%fused_computation.33 | loop fusion | bytes 4194304
  109.1 3.1 %constant_dynamic-update-slice_fusion.1 = bf16[4096,1024]{1,0:T(8,128)(2,1)} fusion(bf16[4096,1024]{1,0:T(8,128)(2,1)} %constant_dynamic-update-slice_fusion.2, bf16[4096,256]{1,0:T(8,128)(2,1)} %collective-permute-done.1), kind=kLoop, calls=%fused_computation.32 | loop fusion | bytes 4194304
  112.2 2.3 copy.96
  115.8 2.7 convert_bitcast_fusion.1
  118.5 3.9 %copy.98 = bf16[8,512,256]{2,1,0:T(8,128)(2,1)} copy(bf16[8,512,256]{1,2,0:T(8,128)(2,1)} %convert_bitcast_fusion.1) | data formatting | bytes 4194304 | tf_op jit(solution)/shard_map/convert_element_type | solution.py:50
  122.4 3.1 %constant_dynamic-update-slice_fusion = bf16[4096,1024]{1,0:T(8,128)(2,1)} fusion(bf16[4096,1024]{1,0:T(8,128)(2,1)} %constant_dynamic-update-slice_fusion.1, bf16[4096,256]{1,0:T(8,128)(2,1)} %collective-permute-done.2), kind=kLoop, calls=%fused_computation.31 | loop fusion | bytes 4194304 | tf_op jit(solution)/shard_map/concatenate | solution.py:38
  125.6 5.9 %convolution_convert_fusion = bf16[4096,256]{1,0:T(8,128)(2,1)S(1)} fusion(bf16[4096,1024]{1,0:T(8,128)(2,1)} %constant_dynamic-update-slice_fusion, bf16[256,1024]{0,1:T(8,128)(2,1)S(1)} %copy-done.8), kind=kOutput, calls=%fused_computation.2 | convolution fusion | flops 2148532224 | bytes 11010048 | tf_op jit(solution)/shard_map/dot_general | solution.py:39
  133.6 4.1 %all-to-all-start.2 = ((bf16[4,512,128]{1,2,0:T(8,128)(2,1)}), bf16[4,512,128]{1,2,0:T(8,128)(2,1)}, u32[]{:S(2)}, u32[]{:S(2)}) async-start(bf16[4,512,128]{1,2,0:T(8,128)(2,1)} %bitcast.33), calls=%async_computation.2 | async-start | bytes 1048576 | tf_op jit(solution)/shard_map/all_to_all | solution.py:80
  137.7 11.4 %copy.99 = bf16[1024,4096]{1,0:T(8,128)(2,1)} copy(bf16[1024,4096]{0,1:T(8,128)(2,1)} %bitcast.25) | data formatting | bytes 16777216 | tf_op jit(solution)/shard_map/dot_general | solution.py:53
  149.1 7.2 %fusion.21 = bf16[256,4,256]{2,0,1:T(8,128)(2,1)} fusion(bf16[4096,256,1]{1,0,2:T(8,128)(2,1)} %bitcast.95, bf16[4,256,4096]{2,1,0:T(8,128)(2,1)} %bitcast.90), kind=kOutput, calls=%fused_computation.42 | convolution fusion | flops 2147483648 | bytes 11010048 | tf_op jit(solution)/shard_map/dot_general | solution.py:53
  163.9 2.6 pad_maximum_fusion
  166.4 2.5 copy.106
  168.9 11.7 %all-to-all-start.3 = ((bf16[64,40,128]{2,1,0:T(8,128)(2,1)}), bf16[64,40,128]{2,1,0:T(8,128)(2,1)S(1)}, u32[]{:S(2)}, u32[]{:S(2)}) async-start(bf16[64,40,128]{2,1,0:T(8,128)(2,1)} %copy.106), calls=%async_computation.3 | async-start | bytes 1310720 | tf_op jit(solution)/shard_map/all_to_all | solution.py:84
  180.6 4.2 %convert_bitcast_fusion.2 = bf16[512,8,256]{0,2,1:T(8,128)(2,1)} fusion(bf16[8,512,256]{2,1,0:T(8,128)(2,1)} %bitcast.106, bf16[512,512]{1,0:T(8,128)(2,1)S(1)} %copy-done), kind=kOutput, calls=%fused_computation.12 | convolution fusion | flops 1074790400 | bytes 4718592 | tf_op jit(solution)/shard_map/mi,kmd->ikd/dot_general | solution.py:43
  184.8 4.5 %copy.87 = bf16[512,8,256]{2,1,0:T(8,128)(2,1)} copy(bf16[512,8,256]{0,2,1:T(8,128)(2,1)} %convert_bitcast_fusion.2) | data formatting | bytes 4194304 | tf_op jit(solution)/shard_map/convert_element_type | solution.py:45
  189.3 11.6 %all-to-all-done.3 = bf16[64,40,128]{2,1,0:T(8,128)(2,1)S(1)} async-done(((bf16[64,40,128]{2,1,0:T(8,128)(2,1)}), bf16[64,40,128]{2,1,0:T(8,128)(2,1)S(1)}, u32[]{:S(2)}, u32[]{:S(2)}) %all-to-all-start.3) | async-done | bytes 655392 | tf_op jit(solution)/shard_map/all_to_all | solution.py:84
  200.9 7.3 %all-to-all-start = ((bf16[512,8,256]{2,1,0:T(8,128)(2,1)}), bf16[512,8,256]{2,1,0:T(8,128)(2,1)}, u32[]{:S(2)}, u32[]{:S(2)}) async-start(bf16[512,8,256]{2,1,0:T(8,128)(2,1)} %copy.87), calls=%async_computation | async-start | bytes 4194304 | tf_op jit(solution)/shard_map/all_to_all | solution.py:46
  208.2 2.9 copy.90
  211.2 45.5 %all-to-all-done = bf16[512,8,256]{2,1,0:T(8,128)(2,1)} async-done(((bf16[512,8,256]{2,1,0:T(8,128)(2,1)}), bf16[512,8,256]{2,1,0:T(8,128)(2,1)}, u32[]{:S(2)}, u32[]{:S(2)}) %all-to-all-start) | async-done | bytes 2097184 | tf_op jit(solution)/shard_map/all_to_all | solution.py:46
  256.7 4.9 %fusion.9 = bf16[512,512]{0,1:T(8,128)(2,1)} fusion(bf16[8,512,256]{2,1,0:T(8,128)(2,1)} %bitcast.89, bf16[8,512,256]{2,1,0:T(8,128)(2,1)} %bitcast.92, bf16[64,8,8,256]{3,2,1,0:T(8,128)(2,1)} %bitcast.39), kind=kOutput, calls=%fused_computation.20 | convolution fusion | flops 1078198272 | bytes 6815744 | tf_op jit(solution)/shard_map/ikd,ijd->kj/dot_general | solution.py:62
  261.6 7.6 %all-to-all-start.4 = ((bf16[4,512,128]{1,2,0:T(8,128)(2,1)}), bf16[4,512,128]{1,2,0:T(8,128)(2,1)S(1)}, u32[]{:S(2)}, u32[]{:S(2)}) async-start(bf16[4,512,128]{1,2,0:T(8,128)(2,1)} %bitcast.104), calls=%async_computation.4 | async-start | bytes 1048576 | tf_op jit(solution)/shard_map/all_to_all | solution.py:80
  270.6 6.6 %all-to-all-done.4 = bf16[4,512,128]{1,2,0:T(8,128)(2,1)S(1)} async-done(((bf16[4,512,128]{1,2,0:T(8,128)(2,1)}), bf16[4,512,128]{1,2,0:T(8,128)(2,1)S(1)}, u32[]{:S(2)}, u32[]{:S(2)}) %all-to-all-start.4) | async-done | bytes 524320 | tf_op jit(solution)/shard_map/all_to_all | solution.py:80
  278.1 6.5 %all-to-all-start.5 = ((bf16[64,8,128]{2,1,0:T(8,128)(2,1)}), bf16[64,8,128]{2,1,0:T(8,128)(2,1)S(1)}, u32[]{:S(2)}, u32[]{:S(2)}) async-start(bf16[64,8,128]{2,1,0:T(8,128)(2,1)} %bitcast.38), calls=%async_computation.5 | async-start | bytes 262144 | tf_op jit(solution)/shard_map/all_to_all | solution.py:84
  284.6 5.7 %fusion.1 = bf16[8,512,256]{1,2,0:T(8,128)(2,1)} fusion(f32[8,512,256]{1,2,0:T(8,128)} %copy.90, bf16[512,512]{1,0:T(8,128)(2,1)} %param.11, bf16[8,512,256]{2,1,0:T(8,128)(2,1)S(1)} %bitcast.93, bf16[64,8,8,256]{3,2,1,0:T(8,128)(2,1)} %bitcast.39), kind=kOutput, calls=%fused_computation.7 | convolution fusion | flops 1080033280 | bytes 11010048 | tf_op jit(solution)/shard_map/kj,ikd->ijd/dot_general | solution.py:63
  290.3 3.9 %copy.91 = bf16[8,512,256]{2,1,0:T(8,128)(2,1)} copy(bf16[8,512,256]{1,2,0:T(8,128)(2,1)} %fusion.1) | data formatting | bytes 4194304 | tf_op jit(solution)/shard_map/convert_element_type | solution.py:68
  (59 shorter events, 25.8 us)
Async XLA Ops:
  0.6 115.2 %copy-start = (bf16[512,512]{1,0:T(8,128)(2,1)S(1)}, bf16[512,512]{1,0:T(8,128)(2,1)}, u32[]{:S(2)}) copy-start(bf16[512,512]{1,0:T(8,128)(2,1)} %param.12) | copy-start | bytes 1572868
  0.6 4.3 %copy-start.2 = (bf16[4096,256]{1,0:T(8,128)(2,1)S(1)}, bf16[4096,256]{1,0:T(8,128)(2,1)}, u32[]{:S(2)}) copy-start(bf16[4096,256]{1,0:T(8,128)(2,1)} %param.8) | copy-start | bytes 6291460
  4.9 3.6 %copy-start.1 = (f32[8,512,256]{1,2,0:T(8,128)S(1)}, f32[8,512,256]{1,2,0:T(8,128)}, u32[]{:S(2)}) copy-start(f32[8,512,256]{1,2,0:T(8,128)} %copy.93) | copy-start | bytes 12582916
  4.9 3.6 %copy-start.7 = (bf16[512,512]{1,0:T(8,128)(2,1)S(1)}, bf16[512,512]{1,0:T(8,128)(2,1)}, u32[]{:S(2)}) copy-start(bf16[512,512]{1,0:T(8,128)(2,1)} %param.11) | copy-start | bytes 1572868
  7.2 1.3 copy-start.3
  15.7 17.2 %copy-start.9 = (bf16[256,1024]{1,0:T(8,128)(2,1)S(1)}, bf16[256,1024]{1,0:T(8,128)(2,1)}, u32[]{:S(2)}) copy-start(bf16[256,1024]{1,0:T(8,128)(2,1)} %param.13) | copy-start | bytes 1572868
  15.7 96.5 %all-to-all-start.1 = ((bf16[8,512,256]{2,0,1:T(8,128)(2,1)}), bf16[8,512,256]{2,0,1:T(8,128)(2,1)}, u32[]{:S(2)}, u32[]{:S(2)}) async-start(bf16[8,512,256]{2,0,1:T(8,128)(2,1)} %copy.94), calls=%async_computation.1 | async-start | bytes 4194304 | tf_op jit(solution)/shard_map/all_to_all | solution.py:33
  31.2 69.8 %collective-permute-start.1 = (bf16[4096,256]{1,0:T(8,128)(2,1)}, bf16[4096,256]{1,0:T(8,128)(2,1)}, u32[]{:S(2)}, u32[]{:S(2)}) collective-permute-start(bf16[4096,256]{1,0:T(8,128)(2,1)} %param.10), channel_id=1, source_target_pairs={{0,2},{1,3},{2,0},{3,1},{4,6},{5,7},{6,4},{7,5},{8,10},{9,11},{10,... | collective-permute-start | bytes 6291464 | tf_op jit(solution)/shard_map/ppermute | solution.py:18
  31.7 74.2 %collective-permute-start = (bf16[4096,256]{1,0:T(8,128)(2,1)}, bf16[4096,256]{1,0:T(8,128)(2,1)}, u32[]{:S(2)}, u32[]{:S(2)}) collective-permute-start(bf16[4096,256]{1,0:T(8,128)(2,1)} %param.10), channel_id=1, source_target_pairs={{0,1},{1,0},{2,3},{3,2},{4,5},{5,4},{6,7},{7,6},{8,9},{9,8},{10,11... | collective-permute-start | bytes 6291464 | tf_op jit(solution)/shard_map/ppermute | solution.py:18
  101.1 21.4 %collective-permute-start.2 = (bf16[4096,256]{1,0:T(8,128)(2,1)}, bf16[4096,256]{1,0:T(8,128)(2,1)}, u32[]{:S(2)}, u32[]{:S(2)}) collective-permute-start(bf16[4096,256]{1,0:T(8,128)(2,1)} %collective-permute-done.1), channel_id=1, source_target_pairs={{0,1},{1,0},{2,3},{3,2},{4,5},{5,4},{6,7},{7,6},{8,9},{9,8},{10,11... | collective-permute-start | bytes 6291464 | tf_op jit(solution)/shard_map/ppermute | solution.py:18
  114.5 1.3 copy-start.5
  122.4 3.2 %copy-start.8 = (bf16[256,1024]{0,1:T(8,128)(2,1)S(1)}, bf16[256,1024]{0,1:T(8,128)(2,1)}, u32[]{:S(2)}) copy-start(bf16[256,1024]{0,1:T(8,128)(2,1)} %bitcast_select_fusion) | copy-start | bytes 1572868
  125.6 5.9 %copy-start.6 = (bf16[64,8,8,256]{3,2,1,0:T(8,128)(2,1)S(1)}, bf16[64,8,8,256]{3,2,1,0:T(8,128)(2,1)}, u32[]{:S(2)}) copy-start(bf16[64,8,8,256]{3,2,1,0:T(8,128)(2,1)} %copy-done.5) | copy-start | bytes 6291460
  131.5 2.1 copy-start.10
  133.6 28.8 %all-to-all-start.2 = ((bf16[4,512,128]{1,2,0:T(8,128)(2,1)}), bf16[4,512,128]{1,2,0:T(8,128)(2,1)}, u32[]{:S(2)}, u32[]{:S(2)}) async-start(bf16[4,512,128]{1,2,0:T(8,128)(2,1)} %bitcast.33), calls=%async_computation.2 | async-start | bytes 1048576 | tf_op jit(solution)/shard_map/all_to_all | solution.py:80
  168.9 32.0 %all-to-all-start.3 = ((bf16[64,40,128]{2,1,0:T(8,128)(2,1)}), bf16[64,40,128]{2,1,0:T(8,128)(2,1)S(1)}, u32[]{:S(2)}, u32[]{:S(2)}) async-start(bf16[64,40,128]{2,1,0:T(8,128)(2,1)} %copy.106), calls=%async_computation.3 | async-start | bytes 1310720 | tf_op jit(solution)/shard_map/all_to_all | solution.py:84
  200.9 55.8 %all-to-all-start = ((bf16[512,8,256]{2,1,0:T(8,128)(2,1)}), bf16[512,8,256]{2,1,0:T(8,128)(2,1)}, u32[]{:S(2)}, u32[]{:S(2)}) async-start(bf16[512,8,256]{2,1,0:T(8,128)(2,1)} %copy.87), calls=%async_computation | async-start | bytes 4194304 | tf_op jit(solution)/shard_map/all_to_all | solution.py:46
  261.6 23.0 %copy-start.4 = (bf16[4096,256]{1,0:T(8,128)(2,1)S(1)}, bf16[4096,256]{1,0:T(8,128)(2,1)}, u32[]{:S(2)}) copy-start(bf16[4096,256]{1,0:T(8,128)(2,1)} %param.9) | copy-start | bytes 6291460
  261.6 15.6 %all-to-all-start.4 = ((bf16[4,512,128]{1,2,0:T(8,128)(2,1)}), bf16[4,512,128]{1,2,0:T(8,128)(2,1)S(1)}, u32[]{:S(2)}, u32[]{:S(2)}) async-start(bf16[4,512,128]{1,2,0:T(8,128)(2,1)} %bitcast.104), calls=%async_computation.4 | async-start | bytes 1048576 | tf_op jit(solution)/shard_map/all_to_all | solution.py:80
  278.1 18.0 %all-to-all-start.5 = ((bf16[64,8,128]{2,1,0:T(8,128)(2,1)}), bf16[64,8,128]{2,1,0:T(8,128)(2,1)S(1)}, u32[]{:S(2)}, u32[]{:S(2)}) async-start(bf16[64,8,128]{2,1,0:T(8,128)(2,1)} %bitcast.38), calls=%async_computation.5 | async-start | bytes 262144 | tf_op jit(solution)/shard_map/all_to_all | solution.py:84

commit v2 on v0

v2 whole, which is shorter than its diff:
```python
import functools

import jax
import jax.numpy as jnp
from jax import lax
from jax.experimental import pallas as pl
from jax.experimental.pallas import tpu as pltpu
from jax.sharding import PartitionSpec as P

ROUNDS = 4
LANES = 128
F32 = jnp.float32
BF16 = jnp.bfloat16


def matmul(left, right):
    return jnp.dot(left, right, preferred_element_type=F32)


def matmul_nt(left, right):
    return lax.dot_general(left, right, (((1,), (1,)), ((), ())), preferred_element_type=F32)


def kernel(
    scale,
    act_hbm, gate_hbm, diag_hbm, cot_hbm, right_hbm, left_hbm, proj_hbm,
    input_grad_hbm, proj_grad_ref, right_grad_ref, left_grad_ref,
    act, gate, diag, cot, fr, fl, proj, frt, flt,
    vals, send1, recv1, mg, send2, recv2, staging, out,
    p_acc, p_send, p_recv,
    l_acc, l_send, l_recv, l2_send, l2_recv,
    r_send, r_recv, r2_send, r2_recv,
    in_sem, out_sem,
    far_send, far_recv, sib_send, sib_recv, fwd_send, fwd_recv,
    s1_send, s1_recv, s2_send, s2_recv,
    p_ssem, p_rsem, l_ssem, l_rsem, l2_ssem, l2_rsem, r_ssem, r_rsem, r2_ssem, r2_rsem,
):
    seq_size = recv1.shape[0]
    lb, block, width = vals.shape
    per_round = lb // ROUNDS
    rows = per_round * lb
    chans = cot.shape[0]
    me = lax.axis_index("seq")
    mc = lax.axis_index("chan")
    sibling = mc + 1 - 2 * lax.rem(mc, 2)
    far = lax.rem(mc + 2, 4)
    far_sibling = 3 - mc

    barrier = pltpu.get_barrier_semaphore()

    def greet(step, carry):
        other = lax.rem(me + step, seq_size)
        pl.semaphore_signal(
            barrier, inc=1, device_id=(other, mc), device_id_type=pl.DeviceIdType.MESH
        )
        return carry

    for other in (sibling, far, far_sibling):
        pl.semaphore_signal(
            barrier, inc=1, device_id=(me, other), device_id_type=pl.DeviceIdType.MESH
        )
    lax.fori_loop(1, seq_size, greet, 0)

    loads = [
        pltpu.make_async_copy(src, dst, in_sem.at[at])
        for at, (src, dst) in enumerate(
            (
                (act_hbm, act),
                (gate_hbm, gate),
                (right_hbm, fr),
                (diag_hbm, diag),
                (cot_hbm, cot.at[mc]),
                (proj_hbm, proj),
                (left_hbm, fl),
            )
        )
    ]
    for load in loads:
        load.start()

    pl.semaphore_wait(barrier, seq_size - 1 + 3)

    def send(src, dst, send_sem, recv_sem, device):
        return pltpu.make_async_remote_copy(
            src_ref=src, dst_ref=dst, send_sem=send_sem, recv_sem=recv_sem,
            device_id=device, device_id_type=pl.DeviceIdType.MESH,
        )

    def drain(ref, sem):
        pltpu.make_async_copy(ref, ref, sem).wait()

    for turn in range(ROUNDS):
        part = pl.ds(turn * per_round, per_round)
        send(
            cot_hbm.at[part], cot.at[mc, part], far_send.at[turn], far_recv.at[turn], (me, far)
        ).start()
    for turn in range(ROUNDS):
        part = pl.ds(turn * per_round, per_round)
        send(
            cot_hbm.at[part], cot.at[mc, part], sib_send.at[turn], sib_recv.at[turn],
            (me, sibling),
        ).start()

    for load in loads[:4]:
        load.wait()

    def first_part(pair, carry):
        pieces = []
        for off in range(2):
            at = pair * 2 + off
            value = (act[at].astype(F32) * gate[at].astype(F32)).astype(BF16)
            vals[at] = value
            made = matmul(fr[...], value) * diag[at].astype(F32)
            pieces.append(made.reshape(seq_size, lb, width))
        send1[:, pl.ds(pl.multiple_of(pair * 2 * lb, 2 * lb), 2 * lb), :] = jnp.concatenate(
            pieces, axis=1
        ).astype(BF16)
        return carry

    lax.fori_loop(0, lb // 2, first_part, 0)

    def first_sends(step, carry):
        other = lax.rem(me + step, seq_size)
        send(send1.at[other], recv1.at[me], s1_send, s1_recv, (other, mc)).start()
        return carry

    lax.fori_loop(1, seq_size, first_sends, 0)
    recv1[me] = send1[me]

    for load in loads[4:]:
        load.wait()
    flt[...] = fl[...].T
    frt[...] = fr[...].T

    for turn in range(ROUNDS):
        part = pl.ds(turn * per_round, per_round)
        drain(cot.at[far, part], far_recv.at[turn])
        forward = send(
            cot.at[far, part], cot.at[far, part], fwd_send.at[turn], fwd_recv.at[turn],
            (me, sibling),
        )
        forward.start()
        drain(cot.at[sibling, part], sib_recv.at[turn])
        drain(cot.at[far_sibling, part], fwd_recv.at[turn])
        pieces = []
        for off in range(per_round):
            at = turn * per_round + off
            total = matmul_nt(cot[0, at], proj[:, :width])
            for c in range(1, chans):
                total += matmul_nt(cot[c, at], proj[:, c * width : (c + 1) * width])
            up = total.astype(BF16)
            mg[at] = up
            pieces.append(matmul(flt[...], up).reshape(seq_size, lb, width))
        send2[turn] = jnp.concatenate(pieces, axis=1).astype(BF16)

        def second_sends(step, carry, turn=turn):
            other = lax.rem(me + step, seq_size)
            send(
                send2.at[turn, other], recv2.at[me, turn], s2_send.at[turn], s2_recv.at[turn],
                (other, mc),
            ).start()
            return carry

        lax.fori_loop(1, seq_size, second_sends, 0)
        recv2[me, turn] = send2[turn, me]

    def stage(blocks):
        flat = blocks.reshape(block * lb, width).astype(F32)
        for part in range(width // LANES):
            staging[part] = flat[:, part * LANES : (part + 1) * LANES]

    def every(at):
        return jnp.concatenate(
            [
                staging[part, pl.ds(at, block, stride=lb), :]
                for part in range(width // LANES)
            ],
            axis=1,
        )

    drain(recv1.at[pl.ds(0, seq_size - 1)], s1_recv)
    stage(recv1[...])
    p_acc[...] = jnp.zeros_like(p_acc)
    l_acc[...] = jnp.zeros_like(l_acc)

    def mixed_part(at, carry):
        got = every(at).astype(BF16)
        l_acc[...] += matmul_nt(mg[at], got)
        mixed = matmul(fl[...], got).astype(BF16).T
        for c in range(chans):
            p_acc[:, c * width : (c + 1) * width] += matmul(mixed, cot[c, at])
        return carry

    lax.fori_loop(0, lb, mixed_part, 0)

    def over_chan(total, sends, recvs, ssem, rsem):
        share = block // chans
        for c in range(chans):
            sends[c] = total[:, c * share : (c + 1) * share].astype(BF16)
        for other in (far, far_sibling, sibling):
            send(sends.at[other], recvs.at[mc], ssem, rsem, (me, other)).start()
        recvs[mc] = sends[mc]

    def over_seq(recvs, rsem, sends2, recvs2, ssem2, rsem2):
        drain(recvs.at[pl.ds(0, chans - 1)], rsem)
        summed = recvs[0].astype(F32)
        for c in range(1, chans):
            summed += recvs[c].astype(F32)
        sends2[...] = summed.reshape(sends2.shape)

        def go(step, carry):
            other = lax.rem(me + step, seq_size)
            send(sends2.at[other], recvs2.at[me], ssem2, rsem2, (other, mc)).start()
            return carry

        lax.fori_loop(1, seq_size, go, 0)
        recvs2[me] = sends2[me]

    over_chan(l_acc, l_send, l_recv, l_ssem, l_rsem)
    share = p_send.shape[1]
    for c in range(chans):
        turned = p_acc[:, c * width : (c + 1) * width].T.astype(BF16)
        p_send[pl.ds(c * (width // share), width // share)] = turned.reshape(
            width // share, share, width
        )

    def proj_sends(step, carry):
        other = lax.rem(me + step, seq_size)
        send(p_send.at[other], p_recv.at[me], p_ssem, p_rsem, (other, mc)).start()
        return carry

    lax.fori_loop(1, seq_size, proj_sends, 0)
    p_recv[me] = p_send[me]
    over_seq(l_recv, l_rsem, l2_send, l2_recv, l2_ssem, l2_rsem)

    for turn in range(ROUNDS):
        drain(recv2.at[pl.ds(0, seq_size - 1), turn], s2_recv.at[turn])
    stage(recv2[...])
    l_acc[...] = jnp.zeros_like(l_acc)

    def right_part(at, carry):
        grad = (every(at) * diag[at].astype(F32)).astype(BF16)
        out[at] = grad
        l_acc[...] += matmul_nt(grad, vals[at])
        return carry

    lax.fori_loop(0, lb, right_part, 0)
    over_chan(l_acc, r_send, r_recv, r_ssem, r_rsem)

    def input_part(at, carry):
        out[at] = (matmul(frt[...], out[at]) * gate[at].astype(F32)).astype(BF16)
        return carry

    lax.fori_loop(0, lb, input_part, 0)
    store = pltpu.make_async_copy(out, input_grad_hbm, out_sem)
    store.start()
    over_seq(r_recv, r_rsem, r2_send, r2_recv, r2_ssem, r2_rsem)

    drain(p_recv.at[pl.ds(0, seq_size - 1)], p_rsem)
    proj_grad_ref[...] = jnp.sum(p_recv[...].astype(F32), axis=0) * (1.0 / block)
    drain(l2_recv.at[pl.ds(0, seq_size - 1)], l2_rsem)
    left_grad_ref[...] = jnp.sum(l2_recv[...], axis=0) * scale
    drain(r2_recv.at[pl.ds(0, seq_size - 1)], r2_rsem)
    right_grad_ref[...] = jnp.sum(r2_recv[...], axis=0) * scale

    store.wait()
    for turn in range(ROUNDS):
        part = pl.ds(turn * per_round, per_round)
        drain(cot.at[mc, part], far_send.at[turn])
        drain(cot.at[mc, part], sib_send.at[turn])
        drain(cot.at[far, part], fwd_send.at[turn])
        drain(send2.at[turn, pl.ds(0, seq_size - 1)], s2_send.at[turn])
    drain(send1.at[pl.ds(0, seq_size - 1)], s1_send)
    drain(p_send.at[pl.ds(0, seq_size - 1)], p_ssem)
    for sends, ssem, sends2, ssem2 in (
        (l_send, l_ssem, l2_send, l2_ssem),
        (r_send, r_ssem, r2_send, r2_ssem),
    ):
        drain(sends.at[pl.ds(0, chans - 1)], ssem)
        drain(sends2.at[pl.ds(0, seq_size - 1)], ssem2)


def on_device(activation, gating, kernel_diag, cotangent, factor_right, factor_left, projection):
    row_count, width = activation.shape
    block = factor_right.shape[0]
    lb = row_count // block
    full = projection.shape[1]
    seq_size = lax.axis_size("seq")
    chans = lax.axis_size("chan")
    cube = (lb, block, width)
    share = full // seq_size
    col = block // chans
    dma = pltpu.SemaphoreType.DMA
    per_round = lb // ROUNDS
    scratch = [
        pltpu.VMEM(cube, BF16),
        pltpu.VMEM(cube, BF16),
        pltpu.VMEM(cube, BF16),
        pltpu.VMEM((chans,) + cube, BF16),
        pltpu.VMEM((block, block), BF16),
        pltpu.VMEM((block, block), BF16),
        pltpu.VMEM((width, full), BF16),
        pltpu.VMEM((block, block), BF16),
        pltpu.VMEM((block, block), BF16),
        pltpu.VMEM(cube, BF16),
        pltpu.VMEM((seq_size, lb * lb, width), BF16),
        pltpu.VMEM((seq_size, lb * lb, width), BF16),
        pltpu.VMEM(cube, BF16),
        pltpu.VMEM((ROUNDS, seq_size, per_round * lb, width), BF16),
        pltpu.VMEM((seq_size, ROUNDS, per_round * lb, width), BF16),
        pltpu.VMEM((width // LANES, block * lb, LANES), F32),
        pltpu.VMEM(cube, BF16),
        pltpu.VMEM((width, full), F32),
        pltpu.VMEM((seq_size, share, width), BF16),
        pltpu.VMEM((seq_size, share, width), BF16),
        pltpu.VMEM((block, block), F32),
        pltpu.VMEM((chans, block, col), BF16),
        pltpu.VMEM((chans, block, col), BF16),
        pltpu.VMEM((seq_size, lb, col), F32),
        pltpu.VMEM((seq_size, lb, col), F32),
        pltpu.VMEM((chans, block, col), BF16),
        pltpu.VMEM((chans, block, col), BF16),
        pltpu.VMEM((seq_size, lb, col), F32),
        pltpu.VMEM((seq_size, lb, col), F32),
        dma((7,)), dma,
        dma((ROUNDS,)), dma((ROUNDS,)), dma((ROUNDS,)), dma((ROUNDS,)),
        dma((ROUNDS,)), dma((ROUNDS,)),
        dma, dma, dma((ROUNDS,)), dma((ROUNDS,)),
    ] + [dma] * 10
    any_space = pl.BlockSpec(memory_space=pl.ANY)
    vmem = pl.BlockSpec(memory_space=pltpu.VMEM)
    input_grad, proj_grad, right_grad, left_grad = pl.pallas_call(
        functools.partial(kernel, float((block * full) ** (-0.5))),
        out_shape=[
            jax.ShapeDtypeStruct(cube, BF16),
            jax.ShapeDtypeStruct((share, width), F32),
            jax.ShapeDtypeStruct((lb, col), F32),
            jax.ShapeDtypeStruct((lb, col), F32),
        ],
        in_specs=[any_space] * 7,
        out_specs=[any_space, vmem, vmem, vmem],
        scratch_shapes=scratch,
        compiler_params=pltpu.CompilerParams(
            collective_id=0, has_side_effects=True, vmem_limit_bytes=56 * 1024 * 1024
        ),
        cost_estimate=pl.CostEstimate(
            flops=20 * row_count * block * width, bytes_accessed=12 * row_count * width,
            transcendentals=0,
        ),
        name="monarch_backward",
    )(
        activation.reshape(cube), gating.reshape(cube), kernel_diag.reshape(cube),
        cotangent.reshape(cube), factor_right, factor_left, projection,
    )
    return (input_grad.reshape(row_count, width), proj_grad.T, right_grad, left_grad)


def solution(mesh):
    in_specs = (
        P("seq", "chan"),
        P("seq", "chan"),
        P("seq", "chan"),
        P("seq", "chan"),
        P(),
        P(),
        P("chan", None),
    )
    out_specs = (P("seq", "chan"), P("chan", "seq"), P("seq", "chan"), P("seq", "chan"))
    return jax.shard_map(
        on_device, mesh=mesh, in_specs=in_specs, out_specs=out_specs, check_vma=False
    )
```

time: 802 us -> 151 us (0.19)
  waiting for transfers between devices: 688 us -> 0 us
  Pallas kernels: 0 us -> 145 us
  matrix products: 36.5 us -> 0 us
  starting transfers between devices: 28.3 us -> 0 us
  local copies, waits for them, and re-layouts: 28.8 us -> 4.85 us
  between operations: 13.8 us -> 0.67 us
    psum x1 -> x0, waiting for transfers between devices: 303 us -> none  [on_device(): right_total, left_total = lax.psum((right_part, left_part), ('seq', 'chan'))]
    reduce_scatter x1 -> x0, waiting for transfers between devices: 273 us -> none  [on_device(): lax.psum_scatter(updated, 'seq', scatter_dimension=1, tiled=True)]
    pallas_call x0 -> x1, Pallas kernels: none -> 145 us  [on_device(): pl.pallas_call(functools.partial(kernel, float((block * full) ** (-0.5)))...]
    all_gather x1 -> x0, waiting for transfers between devices: 82 us -> none  [on_device(): portion = lax.all_gather(cotangent, 'chan', axis=1, tiled=True)]
    dot_general x8 -> x0, matrix products: 36.5 us -> none  [the longest x1 8.35 us: contract_rows(): lax.dot_general(left_side, right_side, (((0,), (0,)), ((), ())), preferre...]
    all_to_all x2 -> x0, waiting for transfers between devices: 28.7 us -> none  [the longest x1 28.7 us: on_device(): lax.all_to_all(scaled_grad_out, 'seq', split_axis=0, concat_axis=1, tiled...]
    all_to_all x2 -> x0, starting transfers between devices: 28 us -> none  [the longest x1 15.4 us: on_device(): lax.all_to_all(scaled, 'seq', split_axis=1, concat_axis=0, tiled=True)]
    convert_element_type x4 -> x0, local copies, waits for them, and re-layouts: 15.4 us -> none  [the longest x1 4.57 us: on_device(): scaled = (first_out * kernel_cube).astype(jnp.bfloat16)]
  transfers between devices with their start and end apart: 5 -> 0, of which waited for: 4 -> 0; matrix products, arithmetic and copies ran while one was open for 8% -> 0% of each run, Pallas kernels for 0% -> 0%
where the time goes in v2:
time: 151 us
  Pallas kernels  145 us (96%)
  local copies, waits for them, and re-layouts  4.85 us (3%)
    pallas_call x1, Pallas kernels, on_device(): pl.pallas_call(functools.partial(kernel, float((block * full) ** (-0.5)))...  145 us
    unnamed x10, local copies, waits for them, and re-layouts  4.85 us

profile of v2, /device:TPU:1, one launch (start us, length us, event | category | flops | bytes accessed | tf_op | source)
XLA Modules:
  0.0 150.9 jit_solution(916107905888466478)
XLA Ops:
  0.6 145.3 %monarch_backward.1 = (bf16[8,512,256]{2,1,0:T(8,128)(2,1)}, f32[16,256]{1,0:T(8,128)}, f32[8,128]{1,0:T(8,128)}, f32[8,128]{1,0:T(8,128)}) custom-call(bf16[8,512,256]{2,1,0:T(8,128)(2,1)} %bitcast.8, bf16[8,512,256]{2,1,0:T(8,128)(2,1)} %bitcast.9, bf16[8,512,256]{2,1,0:T(8,128)(2,1)} %bitcast.10, bf16[8,512,256]{2,1,0:T(8,128)(2,1)} %bitcast.11, ...), custom_call_target="tpu_custom_call" | custom-call | flops 10737418240 | bytes 12582912 | tf_op jit(solution)/shard_map/monarch_backward/pallas_call | solution.py:332
  146.0 0.0 copy-start
  146.0 0.0 copy-start.2
  146.0 0.0 copy-start.1
  146.0 3.0 %copy.15 = bf16[4096,256]{1,0:T(8,128)(2,1)} copy(bf16[4096,256]{1,0:T(8,128)(2,1)} %bitcast.6) | data formatting | bytes 4194304
  149.1 0.0 copy-done
  149.1 0.6 copy.16
  149.7 0.0 copy-done.2
  149.7 0.6 copy.17
  150.3 0.0 copy-done.1
  150.3 0.6 copy.18
Async XLA Ops:
  146.0 3.1 %copy-start = (f32[16,256]{1,0:T(8,128)S(1)}, f32[16,256]{1,0:T(8,128)}, u32[]{:S(2)}) copy-start(f32[16,256]{1,0:T(8,128)} %get-tuple-element.9) | copy-start | bytes 49156
  146.0 3.7 %copy-start.2 = (f32[8,128]{1,0:T(8,128)S(1)}, f32[8,128]{1,0:T(8,128)}, u32[]{:S(2)}) copy-start(f32[8,128]{1,0:T(8,128)} %get-tuple-element.18) | copy-start | bytes 12292
  146.0 4.3 %copy-start.1 = (f32[8,128]{1,0:T(8,128)S(1)}, f32[8,128]{1,0:T(8,128)}, u32[]{:S(2)}) copy-start(f32[8,128]{1,0:T(8,128)} %get-tuple-element.19) | copy-start | bytes 12292

commit v3 on v2

v3 whole, which is shorter than its diff:
```python
import functools

import jax
import jax.numpy as jnp
from jax import lax
from jax.experimental import pallas as pl
from jax.experimental.pallas import tpu as pltpu
from jax.sharding import PartitionSpec as P

ROUNDS = 4
LANES = 128
CROSS_AFTER = 2
F32 = jnp.float32
BF16 = jnp.bfloat16


def matmul(left, right):
    return jnp.dot(left, right, preferred_element_type=F32)


def matmul_nt(left, right):
    return lax.dot_general(left, right, (((1,), (1,)), ((), ())), preferred_element_type=F32)


def kernel(
    scale,
    act_hbm, gate_hbm, diag_hbm, cot_hbm, right_hbm, left_hbm, proj_hbm,
    input_grad_hbm, proj_grad_hbm, right_grad_hbm, left_grad_hbm,
    act, gate, diag, cot, fr, fl, proj, frt, flt, diag_turned,
    vals, send1, recv1, mg, send2, recv2, staging, out, out_acc,
    p_acc, p_send, p_xrecv, p_ysend, p_yrecv,
    l_acc, l_send, l_recv, l_ysend, l_yrecv,
    r_acc, r_send, r_recv, r_rows, r_ysend, r_yrecv,
    proj_grad, right_grad, left_grad,
    in_sem, out_sem, small_sem,
    far_send, far_recv, sib_send, sib_recv, fwd_send, fwd_recv,
    s1_send, s1_recv, s2_send, s2_recv, rg_send, rg_recv, lg_send, lg_recv,
    px_sems, py_sems, ly_sems, ry_sems,
):
    seq_size = recv1.shape[0]
    lb, block, width = vals.shape
    per_round = lb // ROUNDS
    rows = per_round * lb
    chans = cot.shape[0]
    me = lax.axis_index("seq")
    mc = lax.axis_index("chan")
    sibling = mc + 1 - 2 * lax.rem(mc, 2)
    far = lax.rem(mc + 2, 4)
    far_sibling = 3 - mc
    half = seq_size // 2
    xs = p_send.shape[0]
    zs = half // xs
    yzs = seq_size // xs
    my_half = me // half
    my_z = lax.rem(me, half) // xs
    my_x = lax.rem(me, xs)
    my_yz = me // xs

    barrier = pltpu.get_barrier_semaphore()

    def greet(step, carry):
        other = lax.rem(me + step, seq_size)
        pl.semaphore_signal(
            barrier, inc=1, device_id=(other, mc), device_id_type=pl.DeviceIdType.MESH
        )
        return carry

    group = [
        (x_off, lax.rem(my_x + x_off, xs), chan)
        for x_off in range(xs)
        for chan in (mc, sibling, far, far_sibling)
        if x_off > 0 or chan is not mc
    ]
    for x_off, x, chan in group:
        if chan is not mc:
            pl.semaphore_signal(
                barrier, inc=1, device_id=(my_yz * xs + x, chan),
                device_id_type=pl.DeviceIdType.MESH,
            )
    lax.fori_loop(1, seq_size, greet, 0)

    loads = [
        pltpu.make_async_copy(src, dst, in_sem.at[at])
        for at, (src, dst) in enumerate(
            (
                (act_hbm, act),
                (gate_hbm, gate),
                (right_hbm, fr),
                (diag_hbm, diag),
                (cot_hbm, cot.at[mc]),
                (proj_hbm, proj),
                (left_hbm, fl),
            )
        )
    ]
    for load in loads:
        load.start()

    pl.semaphore_wait(barrier, seq_size - 1 + xs * (chans - 1))

    def send(src, dst, send_sem, recv_sem, device):
        return pltpu.make_async_remote_copy(
            src_ref=src, dst_ref=dst, send_sem=send_sem, recv_sem=recv_sem,
            device_id=device, device_id_type=pl.DeviceIdType.MESH,
        )

    def drain(ref, sem):
        pltpu.make_async_copy(ref, ref, sem).wait()

    for turn in range(ROUNDS):
        part = pl.ds(turn * per_round, per_round)
        send(
            cot_hbm.at[part], cot.at[mc, part], far_send.at[turn], far_recv.at[turn], (me, far)
        ).start()
    for turn in range(ROUNDS):
        part = pl.ds(turn * per_round, per_round)
        send(
            cot_hbm.at[part], cot.at[mc, part], sib_send.at[turn], sib_recv.at[turn],
            (me, sibling),
        ).start()

    def place(step, cross):
        turn = lax.rem(step, zs)
        z_off = (2 * lax.rem(turn, 2) - 1) * ((turn + 1) // 2)
        x_off = step // zs
        z = lax.rem(my_z + z_off + zs, zs)
        x = lax.rem(my_x + x_off, xs)
        return lax.rem(my_half + cross, 2) * half + z * xs + x

    def first_sends(cross):
        def go(step, carry):
            other = place(step, cross)
            send(send1.at[other], recv1.at[me], s1_send, s1_recv, (other, mc)).start()
            return carry

        lax.fori_loop(1 - cross, half, go, 0)

    def second_sends(turn, cross):
        def go(step, carry):
            other = place(step, cross)
            send(
                send2.at[turn, other], recv2.at[me, turn], s2_send.at[turn], s2_recv.at[turn],
                (other, mc),
            ).start()
            return carry

        lax.fori_loop(1 - cross, half, go, 0)

    for load in loads[:4]:
        load.wait()

    def first_part(pair, carry):
        pieces = []
        for off in range(2):
            at = pair * 2 + off
            value = (act[at].astype(F32) * gate[at].astype(F32)).astype(BF16)
            vals[at] = value
            made = matmul(fr[...], value) * diag[at].astype(F32)
            pieces.append(made.reshape(seq_size, lb, width))
        send1[:, pl.ds(pl.multiple_of(pair * 2 * lb, 2 * lb), 2 * lb), :] = jnp.concatenate(
            pieces, axis=1
        ).astype(BF16)
        return carry

    lax.fori_loop(0, lb // 2, first_part, 0)
    first_sends(0)
    recv1[me] = send1[me]

    for load in loads[4:]:
        load.wait()
    flt[...] = fl[...].T

    def stage(blocks):
        count = blocks.shape[0] * blocks.shape[1]
        flat = blocks.reshape(count, width).astype(F32)
        for part in range(width // LANES):
            staging[part, :count] = flat[:, part * LANES : (part + 1) * LANES]

    def every(start, count, stride):
        return jnp.concatenate(
            [
                staging[part, pl.ds(start, count, stride=stride), :]
                for part in range(width // LANES)
            ],
            axis=1,
        )

    for col in range(block // LANES):
        staging[0, col * block : (col + 1) * block] = fr[
            :, col * LANES : (col + 1) * LANES
        ].astype(F32)
    for kk in range(lb):
        turned = jnp.concatenate(
            [
                staging[0, pl.ds(col * block + kk, seq_size, stride=lb), :]
                for col in range(block // LANES)
            ],
            axis=1,
        )
        frt[:, kk * seq_size : (kk + 1) * seq_size] = turned.T.astype(BF16)
    stage(diag[...])

    def turn_diag(kk, carry):
        diag_turned[kk] = every(kk, block, lb).astype(BF16)
        return carry

    lax.fori_loop(0, lb, turn_diag, 0)

    for turn in range(ROUNDS):
        part = pl.ds(turn * per_round, per_round)
        drain(cot.at[far, part], far_recv.at[turn])
        forward = send(
            cot.at[far, part], cot.at[far, part], fwd_send.at[turn], fwd_recv.at[turn],
            (me, sibling),
        )
        forward.start()
        drain(cot.at[sibling, part], sib_recv.at[turn])
        drain(cot.at[far_sibling, part], fwd_recv.at[turn])
        pieces = []
        for off in range(per_round):
            at = turn * per_round + off
            total = matmul_nt(cot[0, at], proj[:, :width])
            for c in range(1, chans):
                total += matmul_nt(cot[c, at], proj[:, c * width : (c + 1) * width])
            up = total.astype(BF16)
            mg[at] = up
            pieces.append(matmul(flt[...], up).reshape(seq_size, lb, width))
        send2[turn] = jnp.concatenate(pieces, axis=1).astype(BF16)
        second_sends(turn, 0)
        recv2[me, turn] = send2[turn, me]
        if turn == CROSS_AFTER:
            first_sends(1)
            for earlier in range(turn):
                second_sends(earlier, 1)
        if turn >= CROSS_AFTER:
            second_sends(turn, 1)

    drain(recv1.at[pl.ds(0, seq_size - 1)], s1_recv)
    stage(recv1[...])
    p_acc[...] = jnp.zeros_like(p_acc)
    l_acc[...] = jnp.zeros_like(l_acc)

    def mixed_part(at, carry):
        got = every(at, block, lb).astype(BF16)
        l_acc[...] += matmul_nt(mg[at], got)
        mixed = matmul(fl[...], got).astype(BF16).T
        for c in range(chans):
            p_acc[:, c * width : (c + 1) * width] += matmul(mixed, cot[c, at])
        return carry

    lax.fori_loop(0, lb, mixed_part, 0)

    def over_group(sends, recvs, ssem, rsem):
        mine = mc * xs + my_x
        for x_off, x, chan in group:
            send(
                sends.at[chan * xs + x], recvs.at[mine], ssem, rsem, (my_yz * xs + x, chan)
            ).start()
        recvs[mine] = sends[mine]

    def group_sum(recvs, rsem):
        drain(recvs.at[pl.ds(0, xs * chans - 1)], rsem)
        return jnp.sum(recvs[...].astype(F32), axis=0)

    def over_yz(total, sends, recvs, sems):
        sends[...] = total.astype(sends.dtype)

        def go(step, carry):
            other = lax.rem(my_yz + step, yzs)
            send(
                sends.at[other], recvs.at[my_yz], sems.at[0], sems.at[1],
                (other * xs + my_x, mc),
            ).start()
            return carry

        lax.fori_loop(1, yzs, go, 0)
        recvs[my_yz] = sends[my_yz]

    def yz_sum(recvs, sems):
        drain(recvs.at[pl.ds(0, yzs - 1)], sems.at[1])
        return jnp.sum(recvs[...].astype(F32), axis=0)

    col = block // chans
    split = l_acc[...].reshape(yzs, xs, lb, block)
    for c in range(chans):
        for x in range(xs):
            l_send[c * xs + x] = (
                split[:, x, :, c * col : (c + 1) * col].reshape(yzs * lb, col).astype(BF16)
            )
    over_group(l_send, l_recv, lg_send, lg_recv)
    share = p_send.shape[2]
    per_chan = yzs // chans
    for c in range(chans):
        turned = p_acc[:, c * width : (c + 1) * width].T.astype(BF16)
        turned = turned.reshape(per_chan, xs, share, width)
        for x in range(xs):
            p_send[x, c * per_chan : (c + 1) * per_chan] = turned[:, x]
    for x_off in range(1, xs):
        x = lax.rem(my_x + x_off, xs)
        send(
            p_send.at[x], p_xrecv.at[my_x], px_sems.at[0], px_sems.at[1], (my_yz * xs + x, mc)
        ).start()
    p_xrecv[my_x] = p_send[my_x]

    def back(turn):
        drain(recv2.at[pl.ds(0, seq_size - 1), turn], s2_recv.at[turn])
        stage(recv2[:, turn])
        r_acc[...] = jnp.zeros_like(r_acc)
        span = per_round * seq_size

        def go(at, carry):
            grad = jnp.concatenate(
                [
                    every(off * lb + at, seq_size, rows)
                    * diag_turned[
                        turn * per_round + off,
                        pl.ds(pl.multiple_of(at * seq_size, seq_size), seq_size),
                    ].astype(F32)
                    for off in range(per_round)
                ],
                axis=0,
            ).astype(BF16)
            out[at, turn * span : (turn + 1) * span] = grad
            made = matmul_nt(grad, vals[at])
            for c in range(chans):
                r_acc[c] += made[:, c * col : (c + 1) * col]
            return carry

        lax.fori_loop(0, lb, go, 0)
        for c in range(chans):
            for x in range(xs):
                r_send[turn, c * xs + x] = jnp.concatenate(
                    [
                        r_acc[c, pl.ds(off * seq_size + x, yzs, stride=xs), :]
                        for off in range(per_round)
                    ],
                    axis=0,
                ).astype(BF16)
        over_group(r_send.at[turn], r_recv.at[turn], rg_send.at[turn], rg_recv.at[turn])

    def right_rows(turn):
        summed = group_sum(r_recv.at[turn], rg_recv.at[turn])
        for off in range(per_round):
            r_rows[pl.ds(turn * per_round + off, yzs, stride=lb), :] = summed[
                off * yzs : (off + 1) * yzs
            ]

    back(0)
    back(1)
    middle = block // 2

    def early_part(at, carry):
        out_acc[at] = matmul(frt[:, :middle], out[at, :middle])
        return carry

    lax.fori_loop(0, lb, early_part, 0)
    back(2)
    back(3)

    def late_part(at, carry):
        total = out_acc[at] + matmul(frt[:, middle:], out[at, middle:])
        out[at] = (total * gate[at].astype(F32)).astype(BF16)
        pltpu.make_async_copy(out.at[at], input_grad_hbm.at[at], out_sem).start()
        return carry

    lax.fori_loop(0, lb, late_part, 0)
    over_yz(group_sum(l_recv, lg_recv).reshape(l_ysend.shape), l_ysend, l_yrecv, ly_sems)
    drain(p_xrecv.at[pl.ds(0, xs - 1)], px_sems.at[1])
    over_yz(jnp.sum(p_xrecv[...].astype(F32), axis=0), p_ysend, p_yrecv, py_sems)
    for turn in range(ROUNDS):
        right_rows(turn)
    over_yz(r_rows[...].reshape(r_ysend.shape), r_ysend, r_yrecv, ry_sems)

    for turn in range(ROUNDS):
        part = pl.ds(turn * per_round, per_round)
        drain(cot.at[mc, part], far_send.at[turn])
        drain(cot.at[mc, part], sib_send.at[turn])
        drain(cot.at[far, part], fwd_send.at[turn])
        drain(send2.at[turn, pl.ds(0, seq_size - 1)], s2_send.at[turn])
        drain(r_send.at[turn, pl.ds(0, xs * chans - 1)], rg_send.at[turn])
    drain(send1.at[pl.ds(0, seq_size - 1)], s1_send)
    drain(l_send.at[pl.ds(0, xs * chans - 1)], lg_send)
    drain(p_send.at[pl.ds(0, xs - 1)], px_sems.at[0])
    for sends, sems in ((p_ysend, py_sems), (l_ysend, ly_sems), (r_ysend, ry_sems)):
        drain(sends.at[pl.ds(0, yzs - 1)], sems.at[0])
    drain(out, out_sem)
    stores = [
        pltpu.make_async_copy(proj_grad, proj_grad_hbm, small_sem.at[0]),
        pltpu.make_async_copy(left_grad, left_grad_hbm, small_sem.at[1]),
        pltpu.make_async_copy(right_grad, right_grad_hbm, small_sem.at[2]),
    ]
    left_grad[...] = yz_sum(l_yrecv, ly_sems) * scale
    stores[1].start()
    proj_grad[...] = yz_sum(p_yrecv, py_sems) * (1.0 / block)
    stores[0].start()
    right_grad[...] = yz_sum(r_yrecv, ry_sems) * scale
    stores[2].start()
    for store in stores:
        store.wait()


def copy_kernel(*refs):
    srcs, dsts, held, sems = refs[:4], refs[4:8], refs[8:12], refs[12]
    lb = srcs[0].shape[0]
    hops = [(srcs[0].at[at], held[0].at[at], dsts[0].at[at]) for at in range(lb)]
    hops += list(zip(srcs[1:], held[1:], dsts[1:]))
    loads = [pltpu.make_async_copy(a, b, sems.at[0, n]) for n, (a, b, c) in enumerate(hops)]
    stores = [pltpu.make_async_copy(b, c, sems.at[1, n]) for n, (a, b, c) in enumerate(hops)]
    for load in loads:
        load.start()
    for load, store in zip(loads, stores):
        load.wait()
        store.start()
    for store in stores:
        store.wait()


def on_device(activation, gating, kernel_diag, cotangent, factor_right, factor_left, projection):
    row_count, width = activation.shape
    block = factor_right.shape[0]
    lb = row_count // block
    full = projection.shape[1]
    seq_size = lax.axis_size("seq")
    chans = lax.axis_size("chan")
    cube = (lb, block, width)
    share = full // seq_size
    col = block // chans
    xs = min(4, seq_size // 2)
    yzs = seq_size // xs
    dma = pltpu.SemaphoreType.DMA
    per_round = lb // ROUNDS
    span = per_round * seq_size

    def small(*lead):
        return pltpu.VMEM(lead + (lb, col), F32)

    scratch = [
        pltpu.VMEM(cube, BF16),
        pltpu.VMEM(cube, BF16),
        pltpu.VMEM(cube, BF16),
        pltpu.VMEM((chans,) + cube, BF16),
        pltpu.VMEM((block, block), BF16),
        pltpu.VMEM((block, block), BF16),
        pltpu.VMEM((width, full), BF16),
        pltpu.VMEM((block, block), BF16),
        pltpu.VMEM((block, block), BF16),
        pltpu.VMEM(cube, BF16),
        pltpu.VMEM(cube, BF16),
        pltpu.VMEM((seq_size, lb * lb, width), BF16),
        pltpu.VMEM((seq_size, lb * lb, width), BF16),
        pltpu.VMEM(cube, BF16),
        pltpu.VMEM((ROUNDS, seq_size, per_round * lb, width), BF16),
        pltpu.VMEM((seq_size, ROUNDS, per_round * lb, width), BF16),
        pltpu.VMEM((width // LANES, block * lb, LANES), F32),
        pltpu.VMEM(cube, BF16),
        pltpu.VMEM(cube, F32),
        pltpu.VMEM((width, full), F32),
        pltpu.VMEM((xs, yzs, share, width), BF16),
        pltpu.VMEM((xs, yzs, share, width), BF16),
        pltpu.VMEM((yzs, share, width), BF16),
        pltpu.VMEM((yzs, share, width), BF16),
        pltpu.VMEM((block, block), F32),
        pltpu.VMEM((chans * xs, yzs * lb, col), BF16),
        pltpu.VMEM((chans * xs, yzs * lb, col), BF16),
        small(yzs), small(yzs),
        pltpu.VMEM((chans, span, col), F32),
        pltpu.VMEM((ROUNDS, chans * xs, span // xs, col), BF16),
        pltpu.VMEM((ROUNDS, chans * xs, span // xs, col), BF16),
        pltpu.VMEM((yzs * lb, col), F32),
        small(yzs), small(yzs),
        pltpu.VMEM((share, width), F32), small(), small(),
        dma((7,)), dma, dma((3,)),
    ] + [dma((ROUNDS,))] * 6 + [
        dma, dma, dma((ROUNDS,)), dma((ROUNDS,)), dma((ROUNDS,)), dma((ROUNDS,)), dma, dma,
    ] + [dma((2,))] * 4
    any_space = pl.BlockSpec(memory_space=pl.ANY)
    shapes = [
        jax.ShapeDtypeStruct(cube, BF16),
        jax.ShapeDtypeStruct((share, width), F32),
        jax.ShapeDtypeStruct((lb, col), F32),
        jax.ShapeDtypeStruct((lb, col), F32),
    ]
    results = pl.pallas_call(
        functools.partial(kernel, float((block * full) ** (-0.5))),
        out_shape=shapes,
        in_specs=[any_space] * 7,
        out_specs=[any_space] * 4,
        scratch_shapes=scratch,
        compiler_params=pltpu.CompilerParams(
            collective_id=0, has_side_effects=True, vmem_limit_bytes=58 * 1024 * 1024
        ),
        cost_estimate=pl.CostEstimate(
            flops=20 * row_count * block * width, bytes_accessed=12 * row_count * width,
            transcendentals=0,
        ),
        name="monarch_backward",
    )(
        activation.reshape(cube), gating.reshape(cube), kernel_diag.reshape(cube),
        cotangent.reshape(cube), factor_right, factor_left, projection,
    )
    input_grad, proj_grad, right_grad, left_grad = pl.pallas_call(
        copy_kernel,
        out_shape=shapes,
        in_specs=[any_space] * 4,
        out_specs=[any_space] * 4,
        scratch_shapes=[pltpu.VMEM(shape.shape, shape.dtype) for shape in shapes]
        + [dma((2, lb + 3))],
        name="copy_results",
    )(*results)
    return (input_grad.reshape(row_count, width), proj_grad.T, right_grad, left_grad)


def solution(mesh):
    in_specs = (
        P("seq", "chan"),
        P("seq", "chan"),
        P("seq", "chan"),
        P("seq", "chan"),
        P(),
        P(),
        P("chan", None),
    )
    out_specs = (P("seq", "chan"), P("chan", "seq"), P("seq", "chan"), P("seq", "chan"))
    return jax.shard_map(
        on_device, mesh=mesh, in_specs=in_specs, out_specs=out_specs, check_vma=False
    )
```

time: 151 us -> 138 us (0.914)
  Pallas kernels: 145 us -> 137 us
  local copies, waits for them, and re-layouts: 4.85 us -> 0 us
    pallas_call x1, Pallas kernels: 145 us -> 135 us  [on_device(): pl.pallas_call(functools.partial(kernel, float((block * full) ** (-0.5)))...]
    unnamed x10 -> x0, local copies, waits for them, and re-layouts: 4.85 us -> none
    pallas_call x0 -> x1, Pallas kernels: none -> 2.46 us  [on_device(): pl.pallas_call(copy_kernel, out_shape=shapes, in_specs=[any_space] * 4, o...]
where the time goes in v3:
time: 138 us
  Pallas kernels  137 us (99%)
    pallas_call x1, Pallas kernels, on_device(): pl.pallas_call(functools.partial(kernel, float((block * full) ** (-0.5)))...  135 us

profile of v3, /device:TPU:1, one launch (start us, length us, event | category | flops | bytes accessed | tf_op | source)
XLA Modules:
  0.0 137.9 jit_solution(14560751936512619935)
XLA Ops:
  0.6 134.8 %monarch_backward.1 = (bf16[8,512,256]{2,1,0:T(8,128)(2,1)}, f32[16,256]{1,0:T(8,128)}, f32[8,128]{1,0:T(8,128)}, f32[8,128]{1,0:T(8,128)}) custom-call(bf16[8,512,256]{2,1,0:T(8,128)(2,1)} %bitcast.6, bf16[8,512,256]{2,1,0:T(8,128)(2,1)} %bitcast.7, bf16[8,512,256]{2,1,0:T(8,128)(2,1)} %bitcast.8, bf16[8,512,256]{2,1,0:T(8,128)(2,1)} %bitcast.9, ...), custom_call_target="tpu_custom_call" | custom-call | flops 10737418240 | bytes 12582912 | tf_op jit(solution)/shard_map/monarch_backward/pallas_call | solution.py:483
  135.5 2.5 %copy_results.1 = (bf16[8,512,256]{2,1,0:T(8,128)(2,1)}, f32[16,256]{1,0:T(8,128)}, f32[8,128]{1,0:T(8,128)}, f32[8,128]{1,0:T(8,128)}) custom-call(bf16[8,512,256]{2,1,0:T(8,128)(2,1)} %get-tuple-element.12.refs_0_, f32[16,256]{1,0:T(8,128)} %get-tuple-element.13.refs_1_, f32[8,128]{1,0:T(8,128)} %get-tuple-element.14.refs_2_, ...), custom_call_target="tpu_custom_call" | custom-call | tf_op jit(solution)/shard_map/copy_results/pallas_call | solution.py:501

commit v4 on v3

--- a/solution.py
+++ b/solution.py
@@ -9,7 +9,8 @@
 
 ROUNDS = 4
 LANES = 128
-CROSS_AFTER = 2
+FIRST_CROSS = 1
+SECOND_CROSS = 3
 F32 = jnp.float32
 BF16 = jnp.bfloat16
 
@@ -47,6 +48,8 @@
     sibling = mc + 1 - 2 * lax.rem(mc, 2)
     far = lax.rem(mc + 2, 4)
     far_sibling = 3 - mc
+    my_lo = mc // 2
+    my_core = lax.rem(mc, 2)
     half = seq_size // 2
     xs = p_send.shape[0]
     zs = half // xs
@@ -66,17 +69,26 @@
         return carry
 
     group = [
-        (x_off, lax.rem(my_x + x_off, xs), chan)
+        (lax.rem(my_x + x_off, xs), chan)
         for x_off in range(xs)
-        for chan in (mc, sibling, far, far_sibling)
+        for chan in (mc, sibling)
         if x_off > 0 or chan is not mc
     ]
-    for x_off, x, chan in group:
+    for x, chan in group:
         if chan is not mc:
             pl.semaphore_signal(
                 barrier, inc=1, device_id=(my_yz * xs + x, chan),
                 device_id_type=pl.DeviceIdType.MESH,
             )
+
+    def greet_far(step, carry):
+        other = lax.rem(my_yz + step, yzs) * xs + my_x
+        pl.semaphore_signal(
+            barrier, inc=1, device_id=(other, far), device_id_type=pl.DeviceIdType.MESH
+        )
+        return carry
+
+    lax.fori_loop(0, yzs, greet_far, 0)
     lax.fori_loop(1, seq_size, greet, 0)
 
     loads = [
@@ -96,8 +108,6 @@
     for load in loads:
         load.start()
 
-    pl.semaphore_wait(barrier, seq_size - 1 + xs * (chans - 1))
-
     def send(src, dst, send_sem, recv_sem, device):
         return pltpu.make_async_remote_copy(
             src_ref=src, dst_ref=dst, send_sem=send_sem, recv_sem=recv_sem,
@@ -106,18 +116,6 @@
 
     def drain(ref, sem):
         pltpu.make_async_copy(ref, ref, sem).wait()
-
-    for turn in range(ROUNDS):
-        part = pl.ds(turn * per_round, per_round)
-        send(
-            cot_hbm.at[part], cot.at[mc, part], far_send.at[turn], far_recv.at[turn], (me, far)
-        ).start()
-    for turn in range(ROUNDS):
-        part = pl.ds(turn * per_round, per_round)
-        send(
-            cot_hbm.at[part], cot.at[mc, part], sib_send.at[turn], sib_recv.at[turn],
-            (me, sibling),
-        ).start()
 
     def place(step, cross):
         turn = lax.rem(step, zs)
@@ -127,10 +125,14 @@
         x = lax.rem(my_x + x_off, xs)
         return lax.rem(my_half + cross, 2) * half + z * xs + x
 
-    def first_sends(cross):
+    def first_sends(cross, first, count):
+        part = pl.ds(first * lb, count * lb)
+
         def go(step, carry):
             other = place(step, cross)
-            send(send1.at[other], recv1.at[me], s1_send, s1_recv, (other, mc)).start()
+            send(
+                send1.at[other, part], recv1.at[me, part], s1_send, s1_recv, (other, mc)
+            ).start()
             return carry
 
         lax.fori_loop(1 - cross, half, go, 0)
@@ -149,21 +151,30 @@
     for load in loads[:4]:
         load.wait()
 
-    def first_part(pair, carry):
+    for pair in range(lb // 2):
         pieces = []
-        for off in range(2):
-            at = pair * 2 + off
+        for at in (2 * pair, 2 * pair + 1):
             value = (act[at].astype(F32) * gate[at].astype(F32)).astype(BF16)
             vals[at] = value
             made = matmul(fr[...], value) * diag[at].astype(F32)
             pieces.append(made.reshape(seq_size, lb, width))
-        send1[:, pl.ds(pl.multiple_of(pair * 2 * lb, 2 * lb), 2 * lb), :] = jnp.concatenate(
+        send1[:, 2 * pair * lb : (2 * pair + 2) * lb, :] = jnp.concatenate(
             pieces, axis=1
         ).astype(BF16)
-        return carry
-
-    lax.fori_loop(0, lb // 2, first_part, 0)
-    first_sends(0)
+        if pair == 0:
+            pl.semaphore_wait(barrier, seq_size - 1 + xs + yzs)
+            for turn in range(ROUNDS):
+                part = pl.ds(turn * per_round, per_round)
+                send(
+                    cot_hbm.at[part], cot.at[mc, part], far_send.at[turn], far_recv.at[turn], (me, far)
+                ).start()
+            for turn in range(ROUNDS):
+                part = pl.ds(turn * per_round, per_round)
+                send(
+                    cot_hbm.at[part], cot.at[mc, part], sib_send.at[turn], sib_recv.at[turn],
+                    (me, sibling),
+                ).start()
+        first_sends(0, 2 * pair, 2)
     recv1[me] = send1[me]
 
     for load in loads[4:]:
@@ -228,11 +239,12 @@
         send2[turn] = jnp.concatenate(pieces, axis=1).astype(BF16)
         second_sends(turn, 0)
         recv2[me, turn] = send2[turn, me]
-        if turn == CROSS_AFTER:
-            first_sends(1)
+        if turn == FIRST_CROSS:
+            first_sends(1, 0, lb)
+        if turn == SECOND_CROSS:
             for earlier in range(turn):
                 second_sends(earlier, 1)
-        if turn >= CROSS_AFTER:
+        if turn >= SECOND_CROSS:
             second_sends(turn, 1)
 
     drain(recv1.at[pl.ds(0, seq_size - 1)], s1_recv)
@@ -240,51 +252,63 @@
     p_acc[...] = jnp.zeros_like(p_acc)
     l_acc[...] = jnp.zeros_like(l_acc)
 
-    def mixed_part(at, carry):
-        got = every(at, block, lb).astype(BF16)
-        l_acc[...] += matmul_nt(mg[at], got)
-        mixed = matmul(fl[...], got).astype(BF16).T
+    def mixed_part(pair, carry):
+        at = pair * 2
+        got = jnp.concatenate([every(at, block, lb), every(at + 1, block, lb)], axis=1)
+        got = got.astype(BF16)
+        l_acc[...] += matmul_nt(jnp.concatenate([mg[at], mg[at + 1]], axis=1), got)
+        mixed = matmul(fl[...], got).astype(BF16)
+        turned = jnp.concatenate([mixed[:, :width].T, mixed[:, width:].T], axis=1)
         for c in range(chans):
-            p_acc[:, c * width : (c + 1) * width] += matmul(mixed, cot[c, at])
+            p_acc[:, c * width : (c + 1) * width] += matmul(
+                turned, cot[c, pl.ds(at, 2)].reshape(2 * block, width)
+            )
         return carry
 
-    lax.fori_loop(0, lb, mixed_part, 0)
+    lax.fori_loop(0, lb // 2, mixed_part, 0)
 
     def over_group(sends, recvs, ssem, rsem):
-        mine = mc * xs + my_x
-        for x_off, x, chan in group:
+        mine = my_core * xs + my_x
+        for x, chan in group:
             send(
-                sends.at[chan * xs + x], recvs.at[mine], ssem, rsem, (my_yz * xs + x, chan)
+                sends.at[lax.rem(chan, 2) * xs + x], recvs.at[mine], ssem, rsem,
+                (my_yz * xs + x, chan),
             ).start()
         recvs[mine] = sends[mine]
 
     def group_sum(recvs, rsem):
-        drain(recvs.at[pl.ds(0, xs * chans - 1)], rsem)
+        drain(recvs.at[pl.ds(0, 2 * xs - 1)], rsem)
         return jnp.sum(recvs[...].astype(F32), axis=0)
 
-    def over_yz(total, sends, recvs, sems):
+    def over_yz(total, sends, recvs, sems, pair):
         sends[...] = total.astype(sends.dtype)
-
-        def go(step, carry):
-            other = lax.rem(my_yz + step, yzs)
-            send(
-                sends.at[other], recvs.at[my_yz], sems.at[0], sems.at[1],
-                (other * xs + my_x, mc),
-            ).start()
-            return carry
-
-        lax.fori_loop(1, yzs, go, 0)
-        recvs[my_yz] = sends[my_yz]
+        near = my_lo * yzs if pair else 0
+
+        def go(first, chan):
+            def step_to(step, carry):
+                other = lax.rem(my_yz + step, yzs)
+                send(
+                    sends.at[first + other], recvs.at[near + my_yz], sems.at[0], sems.at[1],
+                    (other * xs + my_x, chan),
+                ).start()
+                return carry
+
+            return step_to
+
+        if pair:
+            lax.fori_loop(0, yzs, go((1 - my_lo) * yzs, far), 0)
+        lax.fori_loop(1, yzs, go(near, mc), 0)
+        recvs[near + my_yz] = sends[near + my_yz]
 
     def yz_sum(recvs, sems):
-        drain(recvs.at[pl.ds(0, yzs - 1)], sems.at[1])
+        drain(recvs.at[pl.ds(0, recvs.shape[0] - 1)], sems.at[1])
         return jnp.sum(recvs[...].astype(F32), axis=0)
 
     col = block // chans
     split = l_acc[...].reshape(yzs, xs, lb, block)
     for c in range(chans):
         for x in range(xs):
-            l_send[c * xs + x] = (
+            l_send[c % 2 * xs + x, c // 2] = (
                 split[:, x, :, c * col : (c + 1) * col].reshape(yzs * lb, col).astype(BF16)
             )
     over_group(l_send, l_recv, lg_send, lg_recv)
@@ -308,8 +332,8 @@
         r_acc[...] = jnp.zeros_like(r_acc)
         span = per_round * seq_size
 
-        def go(at, carry):
-            grad = jnp.concatenate(
+        def grad_of(at):
+            return jnp.concatenate(
                 [
                     every(off * lb + at, seq_size, rows)
                     * diag_turned[
@@ -320,16 +344,24 @@
                 ],
                 axis=0,
             ).astype(BF16)
-            out[at, turn * span : (turn + 1) * span] = grad
-            made = matmul_nt(grad, vals[at])
+
+        def go(pair, carry):
+            at = pair * 2
+            grads = [grad_of(at), grad_of(at + 1)]
+            out[at, turn * span : (turn + 1) * span] = grads[0]
+            out[at + 1, turn * span : (turn + 1) * span] = grads[1]
+            made = matmul_nt(
+                jnp.concatenate(grads, axis=1),
+                jnp.concatenate([vals[at], vals[at + 1]], axis=1),
+            )
             for c in range(chans):
                 r_acc[c] += made[:, c * col : (c + 1) * col]
             return carry
 
-        lax.fori_loop(0, lb, go, 0)
+        lax.fori_loop(0, lb // 2, go, 0)
         for c in range(chans):
             for x in range(xs):
-                r_send[turn, c * xs + x] = jnp.concatenate(
+                r_send[turn, c % 2 * xs + x, c // 2] = jnp.concatenate(
                     [
                         r_acc[c, pl.ds(off * seq_size + x, yzs, stride=xs), :]
                         for off in range(per_round)
@@ -340,10 +372,11 @@
 
     def right_rows(turn):
         summed = group_sum(r_recv.at[turn], rg_recv.at[turn])
-        for off in range(per_round):
-            r_rows[pl.ds(turn * per_round + off, yzs, stride=lb), :] = summed[
-                off * yzs : (off + 1) * yzs
-            ]
+        for chip in range(2):
+            for off in range(per_round):
+                r_rows[chip, pl.ds(turn * per_round + off, yzs, stride=lb), :] = summed[
+                    chip, off * yzs : (off + 1) * yzs
+                ]
 
     back(0)
     back(1)
@@ -355,6 +388,9 @@
 
     lax.fori_loop(0, lb, early_part, 0)
     back(2)
+    over_yz(group_sum(l_recv, lg_recv).reshape(l_ysend.shape), l_ysend, l_yrecv, ly_sems, True)
+    drain(p_xrecv.at[pl.ds(0, xs - 1)], px_sems.at[1])
+    over_yz(jnp.sum(p_xrecv[...].astype(F32), axis=0), p_ysend, p_yrecv, py_sems, False)
     back(3)
 
     def late_part(at, carry):
@@ -364,12 +400,9 @@
         return carry
 
     lax.fori_loop(0, lb, late_part, 0)
-    over_yz(group_sum(l_recv, lg_recv).reshape(l_ysend.shape), l_ysend, l_yrecv, ly_sems)
-    drain(p_xrecv.at[pl.ds(0, xs - 1)], px_sems.at[1])
-    over_yz(jnp.sum(p_xrecv[...].astype(F32), axis=0), p_ysend, p_yrecv, py_sems)
     for turn in range(ROUNDS):
         right_rows(turn)
-    over_yz(r_rows[...].reshape(r_ysend.shape), r_ysend, r_yrecv, ry_sems)
+    over_yz(r_rows[...].reshape(r_ysend.shape), r_ysend, r_yrecv, ry_sems, True)
 
     for turn in range(ROUNDS):
         part = pl.ds(turn * per_round, per_round)
@@ -377,12 +410,12 @@
         drain(cot.at[mc, part], sib_send.at[turn])
         drain(cot.at[far, part], fwd_send.at[turn])
         drain(send2.at[turn, pl.ds(0, seq_size - 1)], s2_send.at[turn])
-        drain(r_send.at[turn, pl.ds(0, xs * chans - 1)], rg_send.at[turn])
+        drain(r_send.at[turn, pl.ds(0, 2 * xs - 1)], rg_send.at[turn])
     drain(send1.at[pl.ds(0, seq_size - 1)], s1_send)
-    drain(l_send.at[pl.ds(0, xs * chans - 1)], lg_send)
+    drain(l_send.at[pl.ds(0, 2 * xs - 1)], lg_send)
     drain(p_send.at[pl.ds(0, xs - 1)], px_sems.at[0])
     for sends, sems in ((p_ysend, py_sems), (l_ysend, ly_sems), (r_ysend, ry_sems)):
-        drain(sends.at[pl.ds(0, yzs - 1)], sems.at[0])
+        drain(sends.at[pl.ds(0, sends.shape[0] - 1)], sems.at[0])
     drain(out, out_sem)
     stores = [
         pltpu.make_async_copy(proj_grad, proj_grad_hbm, small_sem.at[0]),
@@ -460,14 +493,14 @@
         pltpu.VMEM((yzs, share, width), BF16),
         pltpu.VMEM((yzs, share, width), BF16),
         pltpu.VMEM((block, block), F32),
-        pltpu.VMEM((chans * xs, yzs * lb, col), BF16),
-        pltpu.VMEM((chans * xs, yzs * lb, col), BF16),
-        small(yzs), small(yzs),
+        pltpu.VMEM((2 * xs, 2, yzs * lb, col), BF16),
+        pltpu.VMEM((2 * xs, 2, yzs * lb, col), BF16),
+        small(2 * yzs), small(2 * yzs),
         pltpu.VMEM((chans, span, col), F32),
-        pltpu.VMEM((ROUNDS, chans * xs, span // xs, col), BF16),
-        pltpu.VMEM((ROUNDS, chans * xs, span // xs, col), BF16),
-        pltpu.VMEM((yzs * lb, col), F32),
-        small(yzs), small(yzs),
+        pltpu.VMEM((ROUNDS, 2 * xs, 2, span // xs, col), BF16),
+        pltpu.VMEM((ROUNDS, 2 * xs, 2, span // xs, col), BF16),
+        pltpu.VMEM((2, yzs * lb, col), F32),
+        small(2 * yzs), small(2 * yzs),
         pltpu.VMEM((share, width), F32), small(), small(),
         dma((7,)), dma, dma((3,)),
     ] + [dma((ROUNDS,))] * 6 + [

time: 138 us -> 134 us (0.971)
  Pallas kernels: 137 us -> 133 us
    pallas_call x1, Pallas kernels: 135 us -> 130 us  [on_device(): pl.pallas_call(functools.partial(kernel, float((block * full) ** (-0.5)))...]
where the time goes in v4:
time: 134 us; the launch traced here: 133 us
  Pallas kernels  133 us (99%)
    pallas_call x1, Pallas kernels, on_device(): pl.pallas_call(functools.partial(kernel, float((block * full) ** (-0.5)))...  130 us

profile of v4, /device:TPU:1, one launch (start us, length us, event | category | flops | bytes accessed | tf_op | source)
XLA Modules:
  0.0 133.5 jit_solution(12726275558449233871)
XLA Ops:
  0.6 130.4 %monarch_backward.1 = (bf16[8,512,256]{2,1,0:T(8,128)(2,1)}, f32[16,256]{1,0:T(8,128)}, f32[8,128]{1,0:T(8,128)}, f32[8,128]{1,0:T(8,128)}) custom-call(bf16[8,512,256]{2,1,0:T(8,128)(2,1)} %bitcast.6, bf16[8,512,256]{2,1,0:T(8,128)(2,1)} %bitcast.7, bf16[8,512,256]{2,1,0:T(8,128)(2,1)} %bitcast.8, bf16[8,512,256]{2,1,0:T(8,128)(2,1)} %bitcast.9, ...), custom_call_target="tpu_custom_call" | custom-call | flops 10737418240 | bytes 12582912 | tf_op jit(solution)/shard_map/monarch_backward/pallas_call | solution.py:516
  131.0 2.5 %copy_results.1 = (bf16[8,512,256]{2,1,0:T(8,128)(2,1)}, f32[16,256]{1,0:T(8,128)}, f32[8,128]{1,0:T(8,128)}, f32[8,128]{1,0:T(8,128)}) custom-call(bf16[8,512,256]{2,1,0:T(8,128)(2,1)} %get-tuple-element.12.refs_0_, f32[16,256]{1,0:T(8,128)} %get-tuple-element.13.refs_1_, f32[8,128]{1,0:T(8,128)} %get-tuple-element.14.refs_2_, ...), custom_call_target="tpu_custom_call" | custom-call | tf_op jit(solution)/shard_map/copy_results/pallas_call | solution.py:534

commit v5 on v4

--- a/solution.py
+++ b/solution.py
@@ -225,6 +225,9 @@
             (me, sibling),
         )
         forward.start()
+        if turn == SECOND_CROSS:
+            for earlier in range(turn):
+                second_sends(earlier, 1)
         drain(cot.at[sibling, part], sib_recv.at[turn])
         drain(cot.at[far_sibling, part], fwd_recv.at[turn])
         pieces = []
@@ -241,9 +244,6 @@
         recv2[me, turn] = send2[turn, me]
         if turn == FIRST_CROSS:
             first_sends(1, 0, lb)
-        if turn == SECOND_CROSS:
-            for earlier in range(turn):
-                second_sends(earlier, 1)
         if turn >= SECOND_CROSS:
             second_sends(turn, 1)
 
@@ -399,10 +399,11 @@
         pltpu.make_async_copy(out.at[at], input_grad_hbm.at[at], out_sem).start()
         return carry
 
-    lax.fori_loop(0, lb, late_part, 0)
+    lax.fori_loop(0, lb // 2, late_part, 0)
     for turn in range(ROUNDS):
         right_rows(turn)
     over_yz(r_rows[...].reshape(r_ysend.shape), r_ysend, r_yrecv, ry_sems, True)
+    lax.fori_loop(lb // 2, lb, late_part, 0)
 
     for turn in range(ROUNDS):
         part = pl.ds(turn * per_round, per_round)

time: 134 us -> 131 us (0.978)
  Pallas kernels: 133 us -> 130 us
    pallas_call x1, Pallas kernels: 130 us -> 128 us  [on_device(): pl.pallas_call(functools.partial(kernel, float((block * full) ** (-0.5)))...]
where the time goes in v5:
time: 131 us
  Pallas kernels  130 us (99%)
    pallas_call x1, Pallas kernels, on_device(): pl.pallas_call(functools.partial(kernel, float((block * full) ** (-0.5)))...  128 us

profile of v5, /device:TPU:1, one launch (start us, length us, event | category | flops | bytes accessed | tf_op | source)
XLA Modules:
  0.0 131.1 jit_solution(13318332469664964038)
XLA Ops:
  0.6 128.0 %monarch_backward.1 = (bf16[8,512,256]{2,1,0:T(8,128)(2,1)}, f32[16,256]{1,0:T(8,128)}, f32[8,128]{1,0:T(8,128)}, f32[8,128]{1,0:T(8,128)}) custom-call(bf16[8,512,256]{2,1,0:T(8,128)(2,1)} %bitcast.6, bf16[8,512,256]{2,1,0:T(8,128)(2,1)} %bitcast.7, bf16[8,512,256]{2,1,0:T(8,128)(2,1)} %bitcast.8, bf16[8,512,256]{2,1,0:T(8,128)(2,1)} %bitcast.9, ...), custom_call_target="tpu_custom_call" | custom-call | flops 10737418240 | bytes 12582912 | tf_op jit(solution)/shard_map/monarch_backward/pallas_call | solution.py:517
  128.6 2.5 %copy_results.1 = (bf16[8,512,256]{2,1,0:T(8,128)(2,1)}, f32[16,256]{1,0:T(8,128)}, f32[8,128]{1,0:T(8,128)}, f32[8,128]{1,0:T(8,128)}) custom-call(bf16[8,512,256]{2,1,0:T(8,128)(2,1)} %get-tuple-element.12.refs_0_, f32[16,256]{1,0:T(8,128)} %get-tuple-element.13.refs_1_, f32[8,128]{1,0:T(8,128)} %get-tuple-element.14.refs_2_, ...), custom_call_target="tpu_custom_call" | custom-call | tf_op jit(solution)/shard_map/copy_results/pallas_call | solution.py:535

commit v6 on v5

--- a/solution.py
+++ b/solution.py
@@ -240,12 +240,12 @@
             mg[at] = up
             pieces.append(matmul(flt[...], up).reshape(seq_size, lb, width))
         send2[turn] = jnp.concatenate(pieces, axis=1).astype(BF16)
+        if turn >= SECOND_CROSS:
+            second_sends(turn, 1)
         second_sends(turn, 0)
         recv2[me, turn] = send2[turn, me]
         if turn == FIRST_CROSS:
             first_sends(1, 0, lb)
-        if turn >= SECOND_CROSS:
-            second_sends(turn, 1)
 
     drain(recv1.at[pl.ds(0, seq_size - 1)], s1_recv)
     stage(recv1[...])

time: 131 us -> 131 us (level)
  no operation moved by 1% of the time
where the time goes in v6:
time: 131 us
  Pallas kernels  130 us (99%)
    pallas_call x1, Pallas kernels, on_device(): pl.pallas_call(functools.partial(kernel, float((block * full) ** (-0.5)))...  128 us

profile of v6, /device:TPU:1, one launch (start us, length us, event | category | flops | bytes accessed | tf_op | source)
XLA Modules:
  0.0 131.1 jit_solution(11630517171170867337)
XLA Ops:
  0.6 128.0 %monarch_backward.1 = (bf16[8,512,256]{2,1,0:T(8,128)(2,1)}, f32[16,256]{1,0:T(8,128)}, f32[8,128]{1,0:T(8,128)}, f32[8,128]{1,0:T(8,128)}) custom-call(bf16[8,512,256]{2,1,0:T(8,128)(2,1)} %bitcast.6, bf16[8,512,256]{2,1,0:T(8,128)(2,1)} %bitcast.7, bf16[8,512,256]{2,1,0:T(8,128)(2,1)} %bitcast.8, bf16[8,512,256]{2,1,0:T(8,128)(2,1)} %bitcast.9, ...), custom_call_target="tpu_custom_call" | custom-call | flops 10737418240 | bytes 12582912 | tf_op jit(solution)/shard_map/monarch_backward/pallas_call | solution.py:517
  128.6 2.5 %copy_results.1 = (bf16[8,512,256]{2,1,0:T(8,128)(2,1)}, f32[16,256]{1,0:T(8,128)}, f32[8,128]{1,0:T(8,128)}, f32[8,128]{1,0:T(8,128)}) custom-call(bf16[8,512,256]{2,1,0:T(8,128)(2,1)} %get-tuple-element.12.refs_0_, f32[16,256]{1,0:T(8,128)} %get-tuple-element.13.refs_1_, f32[8,128]{1,0:T(8,128)} %get-tuple-element.14.refs_2_, ...), custom_call_target="tpu_custom_call" | custom-call | tf_op jit(solution)/shard_map/copy_results/pallas_call | solution.py:535
